TPU v7x, 128 devices: a whole 4x4x4 slice. The times are simulated.
128 devices in a mesh: row: 16 (over z_lo, x, core), col: 8 (over y, z_hi).
Axes of the slice: x: 4, y: 4, z: 4 (z_hi: 2, z_lo: 2; z = z_hi * 2 + z_lo), core: 2. Of those that a mesh axis runs over, the one named last changes fastest.
Arguments:
- inputs: bfloat16 [2048, 8192], P('row', 'col'), may hold values from -0.875 to 0.875
- upstream: bfloat16 [2048, 8192], P('row', 'col'), may hold values from -0.75 to 0.75
- mask_flags: int32 [2048], P('row'), may hold values from 0 to 1, as said below
- levels: int32 [4], replicated, may hold values from 100 to 1000
- gate_saved: bfloat16 [2048, 14336], P('col', 'row'), may hold values from -8 to 8
- up_saved: bfloat16 [2048, 14336], P('col', 'row'), may hold values from -3 to 3
- gate_weight: bfloat16 [8192, 14336], P('col', 'row'), may hold values from -0.0625 to 0.0625
- up_weight: bfloat16 [8192, 14336], P('col', 'row'), may hold values from -0.0625 to 0.0625
- down_weight: bfloat16 [14336, 8192], P('row', 'col'), may hold values from -0.046875 to 0.046875
Outputs:
- grad_input: bfloat16 [2048, 8192], P('row', 'col')
- grad_gate: bfloat16 [8192, 14336], P('col', 'row')
- grad_up: bfloat16 [8192, 14336], P('col', 'row')
- grad_down: bfloat16 [14336, 8192], P('row', 'col')
Inputs may be any that keep to these rules, and one draw needn't show every extreme that they name: `mask_flags`: the first token of every sequence is masked.
All inputs are finite; a program needn't handle non-finite values.
Results may differ from a plain program's by a relative error of at most 0.03.
Values may be sent and summed in bfloat16 or wider, within the bound.
A program may use at most 128 MiB of HBM per device.

v0:
```python
import jax
import jax.numpy as jnp
from jax import lax
from jax.sharding import PartitionSpec as P

SEQ = 512


def hidden_side(hidden_grad, gate_vals, up_vals):
    gate_f = gate_vals.astype(jnp.float32)
    up_f = up_vals.astype(jnp.float32)
    sigmoid_gate = jax.nn.sigmoid(gate_f)
    silu_gate = sigmoid_gate * gate_f
    hidden = (silu_gate * up_f).astype(jnp.bfloat16)
    gate_grad = (hidden_grad * up_f * sigmoid_gate * (1.0 + gate_f * (1.0 - sigmoid_gate))).astype(
        jnp.bfloat16
    )
    up_grad = (hidden_grad * silu_gate).astype(jnp.bfloat16)
    return (hidden, gate_grad, up_grad)


def shards(
    inputs, upstream, mask_flags, levels, gate_saved, up_saved, gate_weight, up_weight, down_weight
):
    row_count = inputs.shape[0]
    row_devices = lax.axis_size("row")
    position = lax.axis_index("row") * row_count + jnp.arange(row_count, dtype=jnp.int32)
    sequence = position // SEQ
    seq_ids = jnp.arange(levels.shape[0], dtype=jnp.int32)
    chosen = jnp.sum(jnp.where(sequence[:, None] == seq_ids[None, :], levels[None, :], 0), axis=1)
    noise_level = chosen.astype(jnp.float32) / 1000.0
    masked_total = lax.psum(jnp.sum(mask_flags.astype(jnp.float32)), "row")
    loss_scale = jnp.float32(row_count * row_devices) / masked_total
    factor = mask_flags.astype(jnp.float32) / noise_level
    weighted = (upstream.astype(jnp.float32) * factor[:, None]).astype(jnp.bfloat16)
    all_inputs, all_weighted = (
        lax.all_gather(inputs, "row", axis=0, tiled=True),
        lax.all_gather(weighted, "row", axis=0, tiled=True),
    )
    contract_last = (((1,), (1,)), ((), ()))
    contract_first = (((0,), (0,)), ((), ()))
    summed = lax.psum_scatter(
        lax.dot_general(
            all_weighted, down_weight, contract_last, preferred_element_type=jnp.float32
        ).astype(jnp.bfloat16),
        "col",
        scatter_dimension=0,
        tiled=True,
    ).astype(jnp.float32)
    hidden_grad = loss_scale * summed
    hidden_part, gate_part, up_part = hidden_side(hidden_grad, gate_saved, up_saved)
    hidden, gate_grad, up_grad = (
        lax.all_gather(hidden_part, "col", axis=0, tiled=True),
        lax.all_gather(gate_part, "col", axis=0, tiled=True),
        lax.all_gather(up_part, "col", axis=0, tiled=True),
    )
    grad_down = (
        loss_scale
        * lax.dot_general(hidden, all_weighted, contract_first, preferred_element_type=jnp.float32)
    ).astype(jnp.bfloat16)
    grad_gate = lax.dot_general(
        all_inputs, gate_grad, contract_first, preferred_element_type=jnp.float32
    ).astype(jnp.bfloat16)
    grad_up = lax.dot_general(
        all_inputs, up_grad, contract_first, preferred_element_type=jnp.float32
    ).astype(jnp.bfloat16)
    first_part = lax.dot_general(
        gate_grad, gate_weight, contract_last, preferred_element_type=jnp.float32
    )
    second_part = lax.dot_general(
        up_grad, up_weight, contract_last, preferred_element_type=jnp.float32
    )
    grad_input = lax.psum_scatter(
        (first_part + second_part).astype(jnp.bfloat16), "row", scatter_dimension=0, tiled=True
    )
    return (grad_input, grad_gate, grad_up, grad_down)


def solution(mesh):
    placed = (
        P("row", "col"),
        P("row", "col"),
        P("row"),
        P(),
        P("col", "row"),
        P("col", "row"),
        P("col", "row"),
        P("col", "row"),
        P("row", "col"),
    )
    return jax.shard_map(
        shards,
        mesh=mesh,
        in_specs=placed,
        out_specs=(P("row", "col"), P("col", "row"), P("col", "row"), P("row", "col")),
        check_vma=False,
    )
```

profile of v0, /device:TPU:1, one launch (start us, length us, event | category | flops | bytes accessed | tf_op | source)
XLA Modules:
  0.0 459.2 jit_solution(16077940042158687593)
XLA Ops:
  7.2 0.0 all-gather.6.cloned.1.call-start
  7.2 0.9 select_reduce_fusion
  8.1 1.3 convert_reduce_fusion
  9.4 1.8 multiply_convert_fusion.2
  11.1 0.0 all-gather.6.cloned.1.call-update
  11.2 0.0 reduce-scatter.3.cloned.1.call-start
  11.2 41.2 %all-gather.6.cloned.1.call-done = bf16[2048,1024]{1,0:T(8,128)(2,1)} async-done(((bf16[128,1024]{1,0:T(8,128)(2,1)}), bf16[2048,1024]{1,0:T(8,128)(2,1)}) %all-gather.6.cloned.1.call-update) | async-done | bytes 4194320 | tf_op jit(solution)/shard_map/all_gather | solution.py:38
  52.4 9.1 %convolution_convert_fusion = bf16[2048,896]{1,0:T(8,128)(2,1)} fusion(bf16[2048,1024]{1,0:T(8,128)(2,1)} %all-gather.6.cloned.1.call-done, bf16[896,1024]{1,0:T(8,128)(2,1)} %param.17), kind=kOutput, calls=%fused_computation.2 | convolution fusion | flops 3759931392 | bytes 9699328 | tf_op jit(solution)/shard_map/dot_general | solution.py:43
  61.5 0.0 reduce-scatter.3.cloned.1.call-update
  61.6 0.0 all-gather.8.cloned.1.call-start
  61.6 27.7 %psum.7 = f32[]{:T(128)} all-reduce(f32[]{:T(128)} %get-tuple-element.15), channel_id=1, replica_groups=mesh['row'=16,'col'=8] {'row'}, use_global_device_ids=true, to_apply=%region_1.2 | all-reduce | flops 1 | bytes 8 | tf_op jit(solution)/shard_map/psum | solution.py:32
  90.0 52.6 %reduce-scatter.3.cloned.1.call-done = bf16[256,896]{1,0:T(8,128)(2,1)} async-done(((bf16[2048,896]{1,0:T(8,128)(2,1)}), bf16[256,896]{1,0:T(8,128)(2,1)}) %reduce-scatter.3.cloned.1.call-update) | async-done | bytes 458768 | tf_op jit(solution)/shard_map/reduce_scatter | solution.py:42
  142.6 2.6 fusion.3
  145.2 0.0 all-gather.10.cloned.1.call-start
  145.3 0.5 all-gather.10.cloned.1.call-update
  145.8 0.0 all-gather.12.cloned.1.call-start
  145.9 0.5 all-gather.12.cloned.1.call-update
  146.4 0.0 all-gather.14.cloned.1.call-start
  146.4 0.5 all-gather.14.cloned.1.call-update
  147.0 0.2 reduce-scatter.5.cloned.1.call-start
  147.2 65.8 %all-gather.8.cloned.1.call-done = bf16[2048,896]{1,0:T(8,128)(2,1)} async-done(((bf16[256,896]{1,0:T(8,128)(2,1)}), bf16[2048,896]{1,0:T(8,128)(2,1)}) %all-gather.8.cloned.1.call-update) | async-done | bytes 3670032 | tf_op jit(solution)/shard_map/all_gather | solution.py:54
  213.0 8.9 %fusion.8 = f32[2048,1024]{1,0:T(8,128)} fusion(bf16[2048,896]{1,0:T(8,128)(2,1)} %all-gather.8.cloned.1.call-done, bf16[1024,896]{1,0:T(8,128)(2,1)S(1)} %copy-done), kind=kOutput, calls=%fused_computation.29 | convolution fusion | flops 3758096384 | bytes 13893632 | tf_op jit(solution)/shard_map/dot_general | solution.py:67
  221.9 59.4 %all-gather.10.cloned.1.call-done = bf16[2048,896]{1,0:T(8,128)(2,1)} async-done(((bf16[256,896]{1,0:T(8,128)(2,1)}), bf16[2048,896]{1,0:T(8,128)(2,1)}) %all-gather.10.cloned.1.call-update) | async-done | bytes 3670032 | tf_op jit(solution)/shard_map/all_gather | solution.py:55
  281.2 11.5 %add_convert_fusion = bf16[2048,1024]{1,0:T(8,128)(2,1)} fusion(f32[2048,1024]{1,0:T(8,128)} %fusion.8, bf16[2048,896]{1,0:T(8,128)(2,1)} %all-gather.10.cloned.1.call-done, bf16[1024,896]{1,0:T(8,128)(2,1)} %param.16), kind=kOutput, calls=%fused_computation | convolution fusion | flops 3762290688 | bytes 18087936 | tf_op jit(solution)/shard_map/dot_general | solution.py:70
  292.8 26.1 %all-gather.12.cloned.1.call-done = bf16[2048,1024]{1,0:T(8,128)(2,1)} async-done(((bf16[128,1024]{1,0:T(8,128)(2,1)}), bf16[2048,1024]{1,0:T(8,128)(2,1)}) %all-gather.12.cloned.1.call-update) | async-done | bytes 4194320 | tf_op jit(solution)/shard_map/all_gather | solution.py:37
  318.9 8.5 %convert_bitcast_fusion.1 = bf16[1024,896]{0,1:T(8,128)(2,1)} fusion(bf16[2048,896]{1,0:T(8,128)(2,1)} %all-gather.8.cloned.1.call-done, bf16[2048,1024]{1,0:T(8,128)(2,1)} %all-gather.12.cloned.1.call-done), kind=kOutput, calls=%fused_computation.4 | convolution fusion | flops 3759013888 | bytes 9699328 | tf_op jit(solution)/shard_map/dot_general | solution.py:61
  327.5 3.8 copy.15
  331.3 8.7 %convert_bitcast_fusion = bf16[1024,896]{0,1:T(8,128)(2,1)} fusion(bf16[2048,896]{1,0:T(8,128)(2,1)} %all-gather.10.cloned.1.call-done, bf16[2048,1024]{1,0:T(8,128)(2,1)} %all-gather.12.cloned.1.call-done), kind=kOutput, calls=%fused_computation.3 | convolution fusion | flops 3759013888 | bytes 9699328 | tf_op jit(solution)/shard_map/dot_general | solution.py:64
  340.0 3.8 copy.16
  343.8 44.3 %all-gather.14.cloned.1.call-done = bf16[2048,896]{1,0:T(8,128)(2,1)} async-done(((bf16[256,896]{1,0:T(8,128)(2,1)}), bf16[2048,896]{1,0:T(8,128)(2,1)}) %all-gather.14.cloned.1.call-update) | async-done | bytes 3670032 | tf_op jit(solution)/shard_map/all_gather | solution.py:53
  388.1 8.5 %multiply_convert_fusion = bf16[896,1024]{1,0:T(8,128)(2,1)} fusion(bf16[2048,896]{1,0:T(8,128)(2,1)} %all-gather.14.cloned.1.call-done, bf16[2048,1024]{1,0:T(8,128)(2,1)} %all-gather.6.cloned.1.call-done, f32[]{:T(128)S(6)} %div.27), kind=kOutput, calls=%fused_computation.1 | convolution fusion | flops 3759931392 | bytes 9699332 | tf_op jit(solution)/shard_map/dot_general | solution.py:59
  396.6 55.7 %reduce-scatter.5.cloned.1.call-done = bf16[128,1024]{1,0:T(8,128)(2,1)} async-done(((bf16[2048,1024]{1,0:T(8,128)(2,1)}), bf16[128,1024]{1,0:T(8,128)(2,1)}) %reduce-scatter.5.cloned.1.call-update) | async-done | bytes 262160 | tf_op jit(solution)/shard_map/reduce_scatter | solution.py:73
  (9 shorter events, 0.1 us)
Async XLA Ops:
  7.2 205.8 %copy-start = (bf16[1024,896]{1,0:T(8,128)(2,1)S(1)}, bf16[1024,896]{1,0:T(8,128)(2,1)}, u32[]{:S(2)}) copy-start(bf16[1024,896]{1,0:T(8,128)(2,1)} %param.15) | copy-start | bytes 5505028
  7.2 45.2 %all-gather.6.cloned.1.call-start = ((), (), s32[]{:S(2)}) async-start(), calls=%async_computation.2 | async-start | bytes 4456448 | tf_op jit(solution)/shard_map/all_gather | solution.py:38
  11.2 131.4 %reduce-scatter.3.cloned.1.call-start = ((), (), s32[]{:S(2)}) async-start(), calls=%async_computation.3 | async-start | bytes 4128768 | tf_op jit(solution)/shard_map/reduce_scatter | solution.py:42
  61.5 81.0 %copy-start.1 = (bf16[256,896]{1,0:T(8,128)(2,1)S(1)}, bf16[256,896]{1,0:T(8,128)(2,1)}, u32[]{:S(2)}) copy-start(bf16[256,896]{1,0:T(8,128)(2,1)} %param.14) | copy-start | bytes 1376260
  61.5 81.0 %copy-start.2 = (bf16[256,896]{1,0:T(8,128)(2,1)S(1)}, bf16[256,896]{1,0:T(8,128)(2,1)}, u32[]{:S(2)}) copy-start(bf16[256,896]{1,0:T(8,128)(2,1)} %param.13) | copy-start | bytes 1376260
  61.6 151.4 %all-gather.8.cloned.1.call-start = ((), (), s32[]{:S(2)}) async-start(), calls=%async_computation.4 | async-start | bytes 4128768 | tf_op jit(solution)/shard_map/all_gather | solution.py:54
  145.2 136.0 %all-gather.10.cloned.1.call-start = ((), (), s32[]{:S(2)}) async-start(), calls=%async_computation.5 | async-start | bytes 4128768 | tf_op jit(solution)/shard_map/all_gather | solution.py:55
  145.8 173.1 %all-gather.12.cloned.1.call-start = ((), (), s32[]{:S(2)}) async-start(), calls=%async_computation.7 | async-start | bytes 4456448 | tf_op jit(solution)/shard_map/all_gather | solution.py:37
  146.4 241.7 %all-gather.14.cloned.1.call-start = ((), (), s32[]{:S(2)}) async-start(), calls=%async_computation.8 | async-start | bytes 4128768 | tf_op jit(solution)/shard_map/all_gather | solution.py:53
  147.0 305.4 %reduce-scatter.5.cloned.1.call-start = ((), (), s32[]{:S(2)}) async-start(), calls=%async_computation.6 | async-start | bytes 4456448 | tf_op jit(solution)/shard_map/reduce_scatter | solution.py:73
Sparse Core Ops, SparseCore 0:
  11.3 41.0 all-gather.5
  61.7 80.8 reduce-scatter.2
  145.7 67.2 all-gather.7
  216.0 65.2 all-gather.9
  282.9 35.9 all-gather.11
  321.4 66.6 all-gather.13
  391.2 61.1 reduce-scatter.4
where the time goes:
time: 463 us; the launch traced here: 459 us
  waiting for transfers between devices  347 us (75%)
  matrix products  55.3 us (12%)
  blocking collectives  27.7 us (6%)
  between operations  14.8 us (3%)
  local copies, waits for them, and re-layouts  7.62 us (2%)
  other arithmetic  6.52 us (1%)
    all_gather x1, waiting for transfers between devices, shards(): lax.all_gather(gate_part, 'col', axis=0, tiled=True)  65.8 us
    all_gather x1, waiting for transfers between devices, shards(): lax.all_gather(up_part, 'col', axis=0, tiled=True)  59.4 us
    reduce_scatter x1, waiting for transfers between devices, shards(): lax.psum_scatter((first_part + second_part).astype(jnp.bfloat16), 'row',...  55.7 us
    reduce_scatter x1, waiting for transfers between devices, shards(): lax.psum_scatter(lax.dot_general(all_weighted, down_weight, contract_last...  52.6 us
    all_gather x1, waiting for transfers between devices, shards(): lax.all_gather(hidden_part, 'col', axis=0, tiled=True)  44.3 us
    all_gather x1, waiting for transfers between devices, shards(): lax.all_gather(weighted, 'row', axis=0, tiled=True)  41.2 us
    psum x1, blocking collectives, shards(): masked_total = lax.psum(jnp.sum(mask_flags.astype(jnp.float32)), 'row')  27.7 us
    all_gather x1, waiting for transfers between devices, shards(): lax.all_gather(inputs, 'row', axis=0, tiled=True)  26.1 us
  transfers between devices with their start and end apart: 7, of which 7 were waited for; matrix products, arithmetic and copies ran while one was open for 12% of the time, Pallas kernels for 0%

commit v1 on v0

v1 whole, which is shorter than its diff:
```python
import jax
import jax.numpy as jnp
from jax import lax
from jax.experimental import pallas as pl
from jax.experimental.pallas import tpu as pltpu
from jax.sharding import PartitionSpec as P

SEQ = 512
BF = jnp.bfloat16
F32 = jnp.float32
MESH = pl.DeviceIdType.MESH
NT = (((1,), (1,)), ((), ()))
ORDER = ((2, 1), (2, 0), (1, 1), (-1, 1), (1, 0), (-1, 0), (0, 1), (0, 0))


class Wire:
    def __init__(self, send_sems, recv_sems, anyone):
        self.send_sems, self.recv_sems, self.anyone = send_sems, recv_sems, anyone
        self.count = 0
        self.sent = []

    def new(self):
        self.count += 1
        return self.count - 1

    def copy(self, number, src, dst, device):
        return pltpu.make_async_remote_copy(
            src_ref=src,
            dst_ref=dst,
            send_sem=self.send_sems.at[number],
            recv_sem=self.recv_sems.at[number],
            device_id=device,
            device_id_type=MESH,
        )

    def send(self, number, src, dst, device, keep=True):
        self.copy(number, src, dst, device).start()
        if keep:
            self.sent.append((number, src, dst, device))

    def recv(self, number, dst):
        self.copy(number, dst, dst, self.anyone).wait_recv()

    def drain(self):
        for message in self.sent:
            self.copy(*message).wait_send()


class Gather:
    def __init__(self, wire, buf, slot, minus, plus, across, sibling=None, other_slot=None):
        self.wire, self.buf, self.slot = wire, buf, slot
        self.minus, self.plus, self.across = minus, plus, across
        self.sibling, self.other_slot = sibling, other_slot
        self.ids = {
            name: wire.new()
            for name in ("own_m", "own_p", "own_z", "z_m", "z_p", "fwd_p", "opp_z")
        }
        self.sib_ids = {d: wire.new() for d in ORDER} if sibling is not None else {}

    def push(self, name, d, device):
        ref = self.buf.at[self.slot(d)]
        self.wire.send(self.ids[name], ref, ref, device)

    def share(self, d):
        if self.sibling is not None:
            ref = self.buf.at[self.slot(d)]
            self.wire.send(self.sib_ids[d], ref, ref, self.sibling)

    def take(self, name, d):
        self.wire.recv(self.ids[name], self.buf.at[self.slot(d)])

    def start(self):
        self.push("own_z", (0, 0), self.across)
        self.push("own_m", (0, 0), self.minus)
        self.push("own_p", (0, 0), self.plus)
        self.share((0, 0))

    def z1(self):
        self.take("own_z", (0, 1))
        self.push("z_m", (0, 1), self.minus)
        self.push("z_p", (0, 1), self.plus)
        self.share((0, 1))

    def f1(self):
        self.take("own_p", (-1, 0))
        self.push("fwd_p", (-1, 0), self.plus)
        self.share((-1, 0))

    def rest(self):
        self.take("own_m", (1, 0))
        self.share((1, 0))
        self.take("z_p", (-1, 1))
        self.share((-1, 1))
        self.take("z_m", (1, 1))
        self.share((1, 1))

    def g1(self):
        self.take("fwd_p", (2, 0))
        self.push("opp_z", (2, 0), self.across)
        self.share((2, 0))

    def last(self):
        self.take("opp_z", (2, 1))
        self.share((2, 1))

    def from_sibling(self):
        for d in ORDER:
            self.wire.recv(self.sib_ids[d], self.buf.at[self.other_slot(d)])


class Reduce:
    def __init__(self, wire, part, got, minus, plus, across, keep=True):
        self.wire, self.part, self.got = wire, part, got
        self.minus, self.plus, self.across, self.keep = minus, plus, across, keep
        self.ids = [wire.new() for _ in range(7)]
        self.log = []

    def push(self, index, d, device):
        src = self.part.at[ORDER.index(d)]
        message = (self.ids[index], src, self.got.at[index], device)
        self.wire.send(*message, keep=self.keep)
        self.log.append((index, d, device))

    def drain(self):
        for index, d, device in self.log:
            src = self.part.at[ORDER.index(d)]
            self.wire.copy(self.ids[index], src, self.got.at[index], device).wait_send()

    def add(self, d, *indices):
        term = self.part[ORDER.index(d)].astype(F32)
        for index in indices:
            self.wire.recv(self.ids[index], self.got.at[index])
            term = term + self.got[index].astype(F32)
        return term

    def store(self, d, term):
        self.part[ORDER.index(d)] = term.astype(BF)

    def p0(self):
        self.push(0, (2, 1), self.across)

    def p1(self):
        self.push(2, (1, 1), self.plus)
        self.push(3, (-1, 1), self.minus)

    def p2(self):
        self.push(4, (1, 0), self.plus)

    def t20(self):
        self.store((2, 0), self.add((2, 0), 0))
        self.push(1, (2, 0), self.minus)

    def tm10(self):
        self.store((-1, 0), self.add((-1, 0), 1))
        self.push(5, (-1, 0), self.minus)

    def s01(self):
        self.store((0, 1), self.add((0, 1), 2, 3))
        self.push(6, (0, 1), self.across)

    def final(self):
        return self.add((0, 0), 4, 6, 5)


N_MESSAGES = 2 * 15 + 3 * 2 * 7 + 2 * 7 + 2 * (8 + 7) + 4
N_LOCAL = 10


def kernel(
    levels,
    mask_row,
    inputs,
    upstream,
    gate_saved,
    up_saved,
    gate_weight,
    up_weight,
    down_weight,
    grad_input,
    grad_gate,
    grad_up,
    grad_down,
    w_all,
    in_all,
    h_all,
    g_all,
    u_all,
    gw,
    uw,
    dw,
    up_own,
    in_own,
    gs,
    us,
    h_part,
    h_got,
    q_part,
    q_sib,
    q_got,
    acc_gate,
    acc_up,
    out_gate,
    out_up,
    out_down,
    out_in,
    count,
    send_sems,
    recv_sems,
    local_sems,
):
    row, col = lax.axis_index("row"), lax.axis_index("col")
    z_lo, x, core = row // 8, (row // 2) % 4, row % 2
    y, z_hi = col // 2, col % 2
    sign = 1 - 2 * core

    def row_of(z, x_at, k):
        return z * 8 + lax.rem(x_at + 8, 4) * 2 + k

    def col_of(y_at, z):
        return lax.rem(y_at + 8, 4) * 2 + z

    sibling = (row_of(z_lo, x, 1 - core), col)
    row_z = (row_of(1 - z_lo, x, core), col)
    row_m, row_p = (row_of(z_lo, x - sign, core), col), (row_of(z_lo, x + sign, core), col)
    col_z = (row, col_of(y, 1 - z_hi))
    col_m, col_p = (row, col_of(y - sign, z_hi)), (row, col_of(y + sign, z_hi))

    def flip(bit, d):
        return 1 - bit if d else bit

    def row_slot(d, k=core):
        return row_of(flip(z_lo, d[1]), x + sign * d[0], k)

    def col_slot(d, half):
        return 2 * col_of(y + sign * d[0], flip(z_hi, d[1])) + half

    loads = {}
    for number, (name, src, dst) in enumerate(
        (
            ("upstream", upstream, up_own),
            ("gs", gate_saved, gs),
            ("us", up_saved, us),
            ("inputs", inputs, in_own),
            ("dw", down_weight, dw),
            ("gw", gate_weight, gw),
            ("uw", up_weight, uw),
        )
    ):
        loads[name] = pltpu.make_async_copy(src, dst, local_sems.at[number])
        loads[name].start()

    barrier = pltpu.get_barrier_semaphore()
    neighbours = (sibling, row_z, row_m, row_p, col_z, col_m, col_p)
    for device in neighbours:
        pl.semaphore_signal(barrier, inc=1, device_id=device, device_id_type=MESH)

    flags = jnp.transpose(jnp.broadcast_to(mask_row[...].astype(F32), (128, 128)))
    noise = jnp.full((1, 128), levels[row * 128 // SEQ], jnp.int32).astype(F32) / 1000.0
    factor = flags / noise
    loads["upstream"].wait()
    w_all[row] = (up_own[...].astype(F32) * jnp.concatenate([factor] * 8, axis=1)).astype(BF)
    count[0] = jnp.broadcast_to(jnp.sum(flags, axis=0, keepdims=True), (8, 128))

    pl.semaphore_wait(barrier, len(neighbours))

    wire = Wire(send_sems, recv_sems, sibling)
    gather_w = Gather(wire, w_all, row_slot, row_m, row_p, row_z, sibling, lambda d: row_slot(d, 1 - core))
    gather_i = Gather(wire, in_all, row_slot, row_m, row_p, row_z, sibling, lambda d: row_slot(d, 1 - core))

    def col_gather(buf, half):
        return Gather(wire, buf, lambda d: col_slot(d, half), col_m, col_p, col_z)

    gather_h = [col_gather(h_all, half) for half in range(2)]
    gather_g = [col_gather(g_all, half) for half in range(2)]
    gather_u = [col_gather(u_all, half) for half in range(2)]
    reduce_h = [Reduce(wire, h_part.at[half], h_got.at[half], col_m, col_p, col_z) for half in range(2)]

    step = 1 - 2 * lax.rem(x, 2)
    partners = (
        sibling,
        row_z,
        (row_of(z_lo, x + step, core), col),
        (row_of(z_lo, x - step, core), col),
    )
    count_ids = [wire.new() for _ in partners]

    def count_send(stage):
        wire.send(count_ids[stage], count.at[2 * stage], count.at[2 * stage + 1], partners[stage])

    def count_recv(stage):
        wire.recv(count_ids[stage], count.at[2 * stage + 1])
        count[2 * stage + 2] = count[2 * stage] + count[2 * stage + 1]

    gather_w.start()
    count_send(0)

    def saved(half):
        gate_f = gs[pl.ds(half * 128, 128), :].astype(F32)
        up_f = us[pl.ds(half * 128, 128), :].astype(F32)
        sigmoid_gate = jax.nn.sigmoid(gate_f)
        return gate_f, up_f, sigmoid_gate, sigmoid_gate * gate_f

    loads["gs"].wait()
    loads["us"].wait()
    for half in range(2):
        _, up_f, _, silu_gate = saved(half)
        hidden = (silu_gate * up_f).astype(BF).astype(F32)
        h_all[2 * col + half] = jnp.transpose(hidden).astype(BF)
        gather_h[half].start()
    loads["inputs"].wait()
    in_all[row] = jnp.transpose(in_own[...].astype(F32)).astype(BF)

    gather_w.z1()
    gather_h[0].z1()
    gather_w.f1()
    count_recv(0)
    count_send(1)
    gather_h[1].z1()
    gather_w.rest()
    gather_h[0].f1()
    gather_w.g1()
    gather_h[1].f1()
    gather_h[0].rest()
    gather_w.last()
    gather_w.from_sibling()
    gather_i.start()
    count_recv(1)
    count_send(2)
    loads["dw"].wait()

    def terms(half, pair):
        ds = ORDER[2 * pair : 2 * pair + 2]
        rows = jnp.concatenate([w_all[col_slot(d, half)] for d in ds], axis=0)
        term = lax.dot_general(rows, dw[...], NT, preferred_element_type=F32).astype(BF)
        h_part[half, 2 * pair] = term[:128]
        h_part[half, 2 * pair + 1] = term[128:]

    def hidden_grads(half):
        scale = 2048.0 / count[8][0:1, 0:1]
        hidden_grad = scale * reduce_h[half].final()
        gate_f, up_f, sigmoid_gate, silu_gate = saved(half)
        g_all[2 * col + half] = (
            hidden_grad * up_f * sigmoid_gate * (1.0 + gate_f * (1.0 - sigmoid_gate))
        ).astype(BF)
        gather_g[half].start()
        u_all[2 * col + half] = (hidden_grad * silu_gate).astype(BF)
        gather_u[half].start()

    stores = []

    def store(src, dst):
        stores.append(pltpu.make_async_copy(src, dst, local_sems.at[7 + len(stores)]))
        stores[-1].start()

    def down_tile(tile):
        scale = 2048.0 / count[8][0:1, 0:1]
        at = pl.ds(tile * 448, 448)
        lhs = jnp.concatenate([h_all[slot, at, :] for slot in range(16)], axis=1)
        rhs = jnp.concatenate([w_all[slot] for slot in range(16)], axis=0)
        out_down[at, :] = (scale * jnp.dot(lhs, rhs, preferred_element_type=F32)).astype(BF)

    def weight_tile(half, acc, out, grads, tile):
        at = pl.ds(tile * 512, 512)
        lhs = jnp.concatenate([in_all[2 * c + half, at, :] for c in range(8)], axis=1)
        rhs = jnp.concatenate([grads[2 * c + half] for c in range(8)], axis=0)
        term = jnp.dot(lhs, rhs, preferred_element_type=F32)
        if half == 0:
            acc[at, :] = term
        else:
            out[at, :] = (acc[at, :] + term).astype(BF)

    first, second = reduce_h
    terms(0, 0)
    first.p0()
    terms(0, 1)
    first.p1()
    gather_h[0].g1()
    gather_h[1].rest()
    terms(0, 2)
    first.p2()
    first.t20()
    gather_i.z1()
    terms(0, 3)
    gather_h[1].g1()
    terms(1, 0)
    second.p0()
    terms(1, 1)
    second.p1()
    gather_i.f1()
    count_recv(2)
    count_send(3)
    first.s01()
    first.tm10()
    terms(1, 2)
    second.p2()
    second.t20()
    terms(1, 3)
    gather_i.rest()
    count_recv(3)
    hidden_grads(0)
    second.s01()
    second.tm10()
    gather_h[0].last()
    gather_h[1].last()
    gather_i.g1()
    gather_i.last()
    gather_g[0].z1()
    gather_u[0].z1()
    hidden_grads(1)
    down_tile(0)
    gather_g[0].f1()
    gather_u[0].f1()
    gather_g[1].z1()
    gather_u[1].z1()
    down_tile(1)
    store(out_down, grad_down)
    gather_g[0].rest()
    gather_u[0].rest()
    gather_g[1].f1()
    gather_u[1].f1()
    gather_g[0].g1()
    gather_u[0].g1()
    gather_i.from_sibling()
    loads["gw"].wait()
    loads["uw"].wait()

    class RowReduce:
        def __init__(self, half):
            self.half = half
            self.ids = [wire.new() for _ in ORDER]
            self.ring = Reduce(wire, q_part.at[half], q_got, row_m, row_p, row_z, keep=False)

        def when_owner(self, do):
            pl.when(core == self.half)(do)

        def compute(self, pair):
            slots = [
                row_of(flip(z_lo, d[1]), x + (1 - 2 * self.half) * d[0], self.half)
                for d in ORDER[2 * pair : 2 * pair + 2]
            ]
            gate_rows = jnp.concatenate([g_all[slot] for slot in slots], axis=0)
            up_rows = jnp.concatenate([u_all[slot] for slot in slots], axis=0)
            term = lax.dot_general(gate_rows, gw[...], NT, preferred_element_type=F32)
            term = term + lax.dot_general(up_rows, uw[...], NT, preferred_element_type=F32)
            q_part[self.half, 2 * pair] = term[:128].astype(BF)
            q_part[self.half, 2 * pair + 1] = term[128:].astype(BF)

            @pl.when(core != self.half)
            def _():
                for index in (2 * pair, 2 * pair + 1):
                    wire.send(
                        self.ids[index],
                        q_part.at[self.half, index],
                        q_sib.at[index],
                        sibling,
                        keep=False,
                    )

        def collect(self, pair):
            for index in (2 * pair, 2 * pair + 1):
                wire.recv(self.ids[index], q_sib.at[index])
                q_part[self.half, index] = (
                    q_part[self.half, index].astype(F32) + q_sib[index].astype(F32)
                ).astype(BF)

        def drain(self):
            @pl.when(core != self.half)
            def _():
                for index in range(8):
                    wire.copy(
                        self.ids[index],
                        q_part.at[self.half, index],
                        q_sib.at[index],
                        sibling,
                    ).wait_send()

            self.when_owner(self.ring.drain)

    def row_stage(reduce, pair):
        def do():
            reduce.collect(pair)
            if pair == 0:
                reduce.ring.p0()
            elif pair == 1:
                reduce.ring.p1()
            elif pair == 2:
                reduce.ring.p2()
                reduce.ring.t20()

        reduce.when_owner(do)

    def finish(reduce):
        def do():
            out_in[...] = reduce.ring.final().astype(BF)

        reduce.when_owner(do)

    rows0, rows1 = RowReduce(0), RowReduce(1)

    gather_g[0].last()
    gather_u[0].last()
    rows0.compute(0)
    gather_g[1].rest()
    rows0.compute(1)
    gather_u[1].rest()
    row_stage(rows0, 0)
    rows0.compute(2)
    row_stage(rows0, 1)
    rows0.compute(3)
    row_stage(rows0, 2)
    gather_g[1].g1()
    row_stage(rows0, 3)
    weight_tile(0, acc_gate, out_gate, g_all, 0)
    rows0.when_owner(rows0.ring.s01)
    rows0.when_owner(rows0.ring.tm10)
    gather_u[1].g1()
    weight_tile(0, acc_gate, out_gate, g_all, 1)
    weight_tile(0, acc_up, out_up, u_all, 0)
    weight_tile(0, acc_up, out_up, u_all, 1)
    finish(rows0)

    gather_g[1].last()
    gather_u[1].last()
    rows1.compute(0)
    rows1.compute(1)
    row_stage(rows1, 0)
    rows1.compute(2)
    row_stage(rows1, 1)
    rows1.compute(3)
    row_stage(rows1, 2)
    row_stage(rows1, 3)
    weight_tile(1, acc_gate, out_gate, g_all, 0)
    rows1.when_owner(rows1.ring.s01)
    rows1.when_owner(rows1.ring.tm10)
    weight_tile(1, acc_gate, out_gate, g_all, 1)
    store(out_gate, grad_gate)
    weight_tile(1, acc_up, out_up, u_all, 0)
    weight_tile(1, acc_up, out_up, u_all, 1)
    store(out_up, grad_up)
    finish(rows1)
    last = pltpu.make_async_copy(out_in, grad_input, local_sems.at[3])
    last.start()
    wire.drain()
    rows0.drain()
    rows1.drain()
    for copy in stores:
        copy.wait()
    last.wait()
    assert wire.count == N_MESSAGES, wire.count


def shards(
    inputs, upstream, mask_flags, levels, gate_saved, up_saved, gate_weight, up_weight, down_weight
):
    anywhere = pl.BlockSpec(memory_space=pl.ANY)
    return pl.pallas_call(
        kernel,
        out_shape=(
            jax.ShapeDtypeStruct((128, 1024), BF),
            jax.ShapeDtypeStruct((1024, 896), BF),
            jax.ShapeDtypeStruct((1024, 896), BF),
            jax.ShapeDtypeStruct((896, 1024), BF),
        ),
        in_specs=[
            pl.BlockSpec(memory_space=pltpu.SMEM),
            pl.BlockSpec(memory_space=pltpu.VMEM),
        ]
        + [anywhere] * 7,
        out_specs=(anywhere,) * 4,
        scratch_shapes=[
            pltpu.VMEM((16, 128, 1024), BF),
            pltpu.VMEM((16, 1024, 128), BF),
            pltpu.VMEM((16, 896, 128), BF),
            pltpu.VMEM((16, 128, 896), BF),
            pltpu.VMEM((16, 128, 896), BF),
            pltpu.VMEM((1024, 896), BF),
            pltpu.VMEM((1024, 896), BF),
            pltpu.VMEM((896, 1024), BF),
            pltpu.VMEM((128, 1024), BF),
            pltpu.VMEM((128, 1024), BF),
            pltpu.VMEM((256, 896), BF),
            pltpu.VMEM((256, 896), BF),
            pltpu.VMEM((2, 8, 128, 896), BF),
            pltpu.VMEM((2, 7, 128, 896), BF),
            pltpu.VMEM((2, 8, 128, 1024), BF),
            pltpu.VMEM((8, 128, 1024), BF),
            pltpu.VMEM((7, 128, 1024), BF),
            pltpu.VMEM((1024, 896), F32),
            pltpu.VMEM((1024, 896), F32),
            pltpu.VMEM((1024, 896), BF),
            pltpu.VMEM((1024, 896), BF),
            pltpu.VMEM((896, 1024), BF),
            pltpu.VMEM((128, 1024), BF),
            pltpu.VMEM((9, 8, 128), F32),
            pltpu.SemaphoreType.DMA((N_MESSAGES,)),
            pltpu.SemaphoreType.DMA((N_MESSAGES,)),
            pltpu.SemaphoreType.DMA((N_LOCAL,)),
        ],
        compiler_params=pltpu.CompilerParams(
            collective_id=0, has_side_effects=True, vmem_limit_bytes=62 * 2**20
        ),
        cost_estimate=pl.CostEstimate(
            flops=12 * 2048 * 1024 * 896, bytes_accessed=16 * 2**20, transcendentals=2 * 256 * 896
        ),
        name="swiglu_backward",
    )(
        levels,
        mask_flags.reshape(1, -1),
        inputs,
        upstream,
        gate_saved,
        up_saved,
        gate_weight,
        up_weight,
        down_weight,
    )


def solution(mesh):
    placed = (
        P("row", "col"),
        P("row", "col"),
        P("row"),
        P(),
        P("col", "row"),
        P("col", "row"),
        P("col", "row"),
        P("col", "row"),
        P("row", "col"),
    )
    return jax.shard_map(
        shards,
        mesh=mesh,
        in_specs=placed,
        out_specs=(P("row", "col"), P("col", "row"), P("col", "row"), P("row", "col")),
        check_vma=False,
    )
```

time: 463 us -> 180 us (0.39)
  waiting for transfers between devices: 347 us -> 0 us
  Pallas kernels: 0 us -> 171 us
  matrix products: 55.3 us -> 0 us
  blocking collectives: 27.7 us -> 0 us
  between operations: 14.8 us -> 0.65 us
  other arithmetic: 6.52 us -> 0 us
    all_gather x5 -> x0, waiting for transfers between devices: 237 us -> none  [the longest x1 65.8 us: shards(): lax.all_gather(gate_part, 'col', axis=0, tiled=True)]
    pallas_call x0 -> x1, Pallas kernels: none -> 171 us  [shards(): pl.pallas_call(kernel, out_shape=(jax.ShapeDtypeStruct((128, 1024), BF),...]
    reduce_scatter x2 -> x0, waiting for transfers between devices: 108 us -> none  [the longest x1 55.7 us: shards(): lax.psum_scatter((first_part + second_part).astype(jnp.bfloat16), 'row',...]
    dot_general x6 -> x0, matrix products: 55.3 us -> none  [the longest x1 11.5 us: shards(): lax.dot_general(up_grad, up_weight, contract_last, preferred_element_type...]
    psum x1 -> x0, blocking collectives: 27.7 us -> none  [shards(): masked_total = lax.psum(jnp.sum(mask_flags.astype(jnp.float32)), 'row')]
  transfers between devices with their start and end apart: 7 -> 0, of which waited for: 7 -> 0; matrix products, arithmetic and copies ran while one was open for 12% -> 0% of each run, Pallas kernels for 0% -> 0%
where the time goes in v1:
time: 180 us
  Pallas kernels  171 us (95%)
  local copies, waits for them, and re-layouts  8.07 us (4%)
    pallas_call x1, Pallas kernels, shards(): pl.pallas_call(kernel, out_shape=(jax.ShapeDtypeStruct((128, 1024), BF),...  171 us
    unnamed x8, local copies, waits for them, and re-layouts  8.07 us

profile of v1, /device:TPU:1, one launch (start us, length us, event | category | flops | bytes accessed | tf_op | source)
XLA Modules:
  0.0 179.9 jit_solution(7672825328926065556)
XLA Ops:
  0.6 171.2 %swiglu_backward.1 = (bf16[128,1024]{1,0:T(8,128)(2,1)}, bf16[1024,896]{1,0:T(8,128)(2,1)}, bf16[1024,896]{1,0:T(8,128)(2,1)}, bf16[896,1024]{1,0:T(8,128)(2,1)}) custom-call(s32[4]{0:T(128)} %levels.1, s32[1,128]{1,0:T(1,128)} %bitcast.1, bf16[128,1024]{1,0:T(8,128)(2,1)} %inputs.1, bf16[128,1024]{1,0:T(8,128)(2,1)} %upstream.1, ...), custom_call_target="tpu_custom_call" | custom-call | flops 22548578304 | bytes 16777216 | tf_op jit(solution)/shard_map/swiglu_backward/pallas_call | solution.py:556
  171.9 1.7 copy.17
  173.5 0.0 copy-start.1
  173.5 3.0 %copy.18 = bf16[1024,896]{1,0:T(8,128)(2,1)} copy(bf16[1024,896]{1,0:T(8,128)(2,1)} %get-tuple-element.9) | data formatting | bytes 3670016
  176.5 0.0 copy-done.1
  176.5 0.0 copy-start
  176.5 1.2 copy.19
  177.8 0.9 copy-done
  178.7 1.2 copy.20
Async XLA Ops:
  173.5 3.0 %copy-start.1 = (bf16[1024,896]{1,0:T(8,128)(2,1)S(1)}, bf16[1024,896]{1,0:T(8,128)(2,1)}, u32[]{:S(2)}) copy-start(bf16[1024,896]{1,0:T(8,128)(2,1)} %get-tuple-element.10) | copy-start | bytes 5505028
  176.5 2.2 %copy-start = (bf16[896,1024]{1,0:T(8,128)(2,1)S(1)}, bf16[896,1024]{1,0:T(8,128)(2,1)}, u32[]{:S(2)}) copy-start(bf16[896,1024]{1,0:T(8,128)(2,1)} %get-tuple-element.11) | copy-start | bytes 5505028

commit v2 on v1

--- a/solution.py
+++ b/solution.py
@@ -47,13 +47,16 @@
 
 
 class Gather:
-    def __init__(self, wire, buf, slot, minus, plus, across, sibling=None, other_slot=None):
+    def __init__(
+        self, wire, buf, slot, minus, plus, across, sibling=None, other_slot=None, far_z=True
+    ):
+        self.far_z = far_z
         self.wire, self.buf, self.slot = wire, buf, slot
         self.minus, self.plus, self.across = minus, plus, across
         self.sibling, self.other_slot = sibling, other_slot
         self.ids = {
             name: wire.new()
-            for name in ("own_m", "own_p", "own_z", "z_m", "z_p", "fwd_p", "opp_z")
+            for name in ("own_m", "own_p", "own_z", "z_m", "z_p", "fwd_p", "far")
         }
         self.sib_ids = {d: wire.new() for d in ORDER} if sibling is not None else {}
 
@@ -86,24 +89,33 @@
         self.push("fwd_p", (-1, 0), self.plus)
         self.share((-1, 0))
 
+    def g1(self):
+        if self.far_z:
+            self.take("fwd_p", (2, 0))
+            self.push("far", (2, 0), self.across)
+            self.share((2, 0))
+        else:
+            self.take("z_m", (1, 1))
+            self.push("far", (1, 1), self.minus)
+            self.share((1, 1))
+
     def rest(self):
         self.take("own_m", (1, 0))
         self.share((1, 0))
         self.take("z_p", (-1, 1))
         self.share((-1, 1))
-        self.take("z_m", (1, 1))
-        self.share((1, 1))
-
-    def g1(self):
-        self.take("fwd_p", (2, 0))
-        self.push("opp_z", (2, 0), self.across)
-        self.share((2, 0))
+        if self.far_z:
+            self.take("z_m", (1, 1))
+            self.share((1, 1))
 
     def last(self):
-        self.take("opp_z", (2, 1))
+        if not self.far_z:
+            self.take("fwd_p", (2, 0))
+            self.share((2, 0))
+        self.take("far", (2, 1))
         self.share((2, 1))
 
-    def from_sibling(self):
+    def sib(self):
         for d in ORDER:
             self.wire.recv(self.sib_ids[d], self.buf.at[self.other_slot(d)])
 
@@ -197,6 +209,7 @@
     q_part,
     q_sib,
     q_got,
+    q_acc,
     acc_gate,
     acc_up,
     out_gate,
@@ -264,16 +277,18 @@
     pl.semaphore_wait(barrier, len(neighbours))
 
     wire = Wire(send_sems, recv_sems, sibling)
-    gather_w = Gather(wire, w_all, row_slot, row_m, row_p, row_z, sibling, lambda d: row_slot(d, 1 - core))
-    gather_i = Gather(wire, in_all, row_slot, row_m, row_p, row_z, sibling, lambda d: row_slot(d, 1 - core))
+    def row_gather(buf, far_z):
+        return Gather(
+            wire, buf, row_slot, row_m, row_p, row_z, sibling, lambda d: row_slot(d, 1 - core), far_z
+        )
 
     def col_gather(buf, half):
         return Gather(wire, buf, lambda d: col_slot(d, half), col_m, col_p, col_z)
 
-    gather_h = [col_gather(h_all, half) for half in range(2)]
-    gather_g = [col_gather(g_all, half) for half in range(2)]
-    gather_u = [col_gather(u_all, half) for half in range(2)]
-    reduce_h = [Reduce(wire, h_part.at[half], h_got.at[half], col_m, col_p, col_z) for half in range(2)]
+    W, I = row_gather(w_all, False), row_gather(in_all, False)
+    H0, H1 = (col_gather(h_all, half) for half in range(2))
+    G0, G1 = (col_gather(g_all, half) for half in range(2))
+    U0, U1 = (col_gather(u_all, half) for half in range(2))
 
     step = 1 - 2 * lax.rem(x, 2)
     partners = (
@@ -291,60 +306,41 @@
         wire.recv(count_ids[stage], count.at[2 * stage + 1])
         count[2 * stage + 2] = count[2 * stage] + count[2 * stage + 1]
 
-    gather_w.start()
-    count_send(0)
-
     def saved(half):
         gate_f = gs[pl.ds(half * 128, 128), :].astype(F32)
         up_f = us[pl.ds(half * 128, 128), :].astype(F32)
         sigmoid_gate = jax.nn.sigmoid(gate_f)
         return gate_f, up_f, sigmoid_gate, sigmoid_gate * gate_f
 
-    loads["gs"].wait()
-    loads["us"].wait()
-    for half in range(2):
+    def hidden(half, gather):
         _, up_f, _, silu_gate = saved(half)
-        hidden = (silu_gate * up_f).astype(BF).astype(F32)
-        h_all[2 * col + half] = jnp.transpose(hidden).astype(BF)
-        gather_h[half].start()
-    loads["inputs"].wait()
-    in_all[row] = jnp.transpose(in_own[...].astype(F32)).astype(BF)
-
-    gather_w.z1()
-    gather_h[0].z1()
-    gather_w.f1()
-    count_recv(0)
-    count_send(1)
-    gather_h[1].z1()
-    gather_w.rest()
-    gather_h[0].f1()
-    gather_w.g1()
-    gather_h[1].f1()
-    gather_h[0].rest()
-    gather_w.last()
-    gather_w.from_sibling()
-    gather_i.start()
-    count_recv(1)
-    count_send(2)
-    loads["dw"].wait()
-
-    def terms(half, pair):
-        ds = ORDER[2 * pair : 2 * pair + 2]
-        rows = jnp.concatenate([w_all[col_slot(d, half)] for d in ds], axis=0)
-        term = lax.dot_general(rows, dw[...], NT, preferred_element_type=F32).astype(BF)
-        h_part[half, 2 * pair] = term[:128]
-        h_part[half, 2 * pair + 1] = term[128:]
-
-    def hidden_grads(half):
+        values = (silu_gate * up_f).astype(BF).astype(F32)
+        h_all[2 * col + half] = jnp.transpose(values).astype(BF)
+        gather.start()
+
+    class ColReduce(Reduce):
+        def __init__(self, half):
+            self.half = half
+            super().__init__(wire, h_part.at[half], h_got.at[half], col_m, col_p, col_z)
+
+        def c(self, pair):
+            ds = ORDER[2 * pair : 2 * pair + 2]
+            rows = jnp.concatenate([w_all[col_slot(d, self.half)] for d in ds], axis=0)
+            term = lax.dot_general(rows, dw[...], NT, preferred_element_type=F32).astype(BF)
+            h_part[self.half, 2 * pair] = term[:128]
+            h_part[self.half, 2 * pair + 1] = term[128:]
+            if pair < 3:
+                (self.p0, self.p1, self.p2)[pair]()
+
+    def hidden_grads(half, reduce, gather):
         scale = 2048.0 / count[8][0:1, 0:1]
-        hidden_grad = scale * reduce_h[half].final()
+        hidden_grad = scale * reduce.final()
         gate_f, up_f, sigmoid_gate, silu_gate = saved(half)
         g_all[2 * col + half] = (
             hidden_grad * up_f * sigmoid_gate * (1.0 + gate_f * (1.0 - sigmoid_gate))
         ).astype(BF)
-        gather_g[half].start()
+        gather.start()
         u_all[2 * col + half] = (hidden_grad * silu_gate).astype(BF)
-        gather_u[half].start()
 
     stores = []
 
@@ -352,14 +348,16 @@
         stores.append(pltpu.make_async_copy(src, dst, local_sems.at[7 + len(stores)]))
         stores[-1].start()
 
-    def down_tile(tile):
+    def down(tile):
         scale = 2048.0 / count[8][0:1, 0:1]
-        at = pl.ds(tile * 448, 448)
+        at = pl.ds(tile * 224, 224)
         lhs = jnp.concatenate([h_all[slot, at, :] for slot in range(16)], axis=1)
         rhs = jnp.concatenate([w_all[slot] for slot in range(16)], axis=0)
         out_down[at, :] = (scale * jnp.dot(lhs, rhs, preferred_element_type=F32)).astype(BF)
-
-    def weight_tile(half, acc, out, grads, tile):
+        if tile == 3:
+            store(out_down, grad_down)
+
+    def weight(half, tile, grads, acc, out, result):
         at = pl.ds(tile * 512, 512)
         lhs = jnp.concatenate([in_all[2 * c + half, at, :] for c in range(8)], axis=1)
         rhs = jnp.concatenate([grads[2 * c + half] for c in range(8)], axis=0)
@@ -368,61 +366,8 @@
             acc[at, :] = term
         else:
             out[at, :] = (acc[at, :] + term).astype(BF)
-
-    first, second = reduce_h
-    terms(0, 0)
-    first.p0()
-    terms(0, 1)
-    first.p1()
-    gather_h[0].g1()
-    gather_h[1].rest()
-    terms(0, 2)
-    first.p2()
-    first.t20()
-    gather_i.z1()
-    terms(0, 3)
-    gather_h[1].g1()
-    terms(1, 0)
-    second.p0()
-    terms(1, 1)
-    second.p1()
-    gather_i.f1()
-    count_recv(2)
-    count_send(3)
-    first.s01()
-    first.tm10()
-    terms(1, 2)
-    second.p2()
-    second.t20()
-    terms(1, 3)
-    gather_i.rest()
-    count_recv(3)
-    hidden_grads(0)
-    second.s01()
-    second.tm10()
-    gather_h[0].last()
-    gather_h[1].last()
-    gather_i.g1()
-    gather_i.last()
-    gather_g[0].z1()
-    gather_u[0].z1()
-    hidden_grads(1)
-    down_tile(0)
-    gather_g[0].f1()
-    gather_u[0].f1()
-    gather_g[1].z1()
-    gather_u[1].z1()
-    down_tile(1)
-    store(out_down, grad_down)
-    gather_g[0].rest()
-    gather_u[0].rest()
-    gather_g[1].f1()
-    gather_u[1].f1()
-    gather_g[0].g1()
-    gather_u[0].g1()
-    gather_i.from_sibling()
-    loads["gw"].wait()
-    loads["uw"].wait()
+            if tile == 1:
+                store(out, result)
 
     class RowReduce:
         def __init__(self, half):
@@ -433,15 +378,22 @@
         def when_owner(self, do):
             pl.when(core == self.half)(do)
 
-        def compute(self, pair):
+        def rows(self, grads, pair):
             slots = [
                 row_of(flip(z_lo, d[1]), x + (1 - 2 * self.half) * d[0], self.half)
                 for d in ORDER[2 * pair : 2 * pair + 2]
             ]
-            gate_rows = jnp.concatenate([g_all[slot] for slot in slots], axis=0)
-            up_rows = jnp.concatenate([u_all[slot] for slot in slots], axis=0)
-            term = lax.dot_general(gate_rows, gw[...], NT, preferred_element_type=F32)
-            term = term + lax.dot_general(up_rows, uw[...], NT, preferred_element_type=F32)
+            return jnp.concatenate([grads[slot] for slot in slots], axis=0)
+
+        def a(self, pair):
+            q_acc[pair] = lax.dot_general(
+                self.rows(g_all, pair), gw[...], NT, preferred_element_type=F32
+            )
+
+        def c(self, pair):
+            term = q_acc[pair] + lax.dot_general(
+                self.rows(u_all, pair), uw[...], NT, preferred_element_type=F32
+            )
             q_part[self.half, 2 * pair] = term[:128].astype(BF)
             q_part[self.half, 2 * pair + 1] = term[128:].astype(BF)
 
@@ -456,12 +408,32 @@
                         keep=False,
                     )
 
-        def collect(self, pair):
-            for index in (2 * pair, 2 * pair + 1):
-                wire.recv(self.ids[index], q_sib.at[index])
-                q_part[self.half, index] = (
-                    q_part[self.half, index].astype(F32) + q_sib[index].astype(F32)
-                ).astype(BF)
+        def k(self, pair):
+            def do():
+                for index in (2 * pair, 2 * pair + 1):
+                    wire.recv(self.ids[index], q_sib.at[index])
+                    q_part[self.half, index] = (
+                        q_part[self.half, index].astype(F32) + q_sib[index].astype(F32)
+                    ).astype(BF)
+                if pair < 3:
+                    (self.ring.p0, self.ring.p1, self.ring.p2)[pair]()
+
+            self.when_owner(do)
+
+        def t20(self):
+            self.when_owner(self.ring.t20)
+
+        def tm10(self):
+            self.when_owner(self.ring.tm10)
+
+        def s01(self):
+            self.when_owner(self.ring.s01)
+
+        def fin(self):
+            def do():
+                out_in[...] = self.ring.final().astype(BF)
+
+            self.when_owner(do)
 
         def drain(self):
             @pl.when(core != self.half)
@@ -476,91 +448,180 @@
 
             self.when_owner(self.ring.drain)
 
-    def row_stage(reduce, pair):
-        def do():
-            reduce.collect(pair)
-            if pair == 0:
-                reduce.ring.p0()
-            elif pair == 1:
-                reduce.ring.p1()
-            elif pair == 2:
-                reduce.ring.p2()
-                reduce.ring.t20()
-
-        reduce.when_owner(do)
-
-    def finish(reduce):
-        def do():
-            out_in[...] = reduce.ring.final().astype(BF)
-
-        reduce.when_owner(do)
-
-    rows0, rows1 = RowReduce(0), RowReduce(1)
-
-    gather_g[0].last()
-    gather_u[0].last()
-    rows0.compute(0)
-    gather_g[1].rest()
-    rows0.compute(1)
-    gather_u[1].rest()
-    row_stage(rows0, 0)
-    rows0.compute(2)
-    row_stage(rows0, 1)
-    rows0.compute(3)
-    row_stage(rows0, 2)
-    gather_g[1].g1()
-    row_stage(rows0, 3)
-    weight_tile(0, acc_gate, out_gate, g_all, 0)
-    rows0.when_owner(rows0.ring.s01)
-    rows0.when_owner(rows0.ring.tm10)
-    gather_u[1].g1()
-    weight_tile(0, acc_gate, out_gate, g_all, 1)
-    weight_tile(0, acc_up, out_up, u_all, 0)
-    weight_tile(0, acc_up, out_up, u_all, 1)
-    finish(rows0)
-
-    gather_g[1].last()
-    gather_u[1].last()
-    rows1.compute(0)
-    rows1.compute(1)
-    row_stage(rows1, 0)
-    rows1.compute(2)
-    row_stage(rows1, 1)
-    rows1.compute(3)
-    row_stage(rows1, 2)
-    row_stage(rows1, 3)
-    weight_tile(1, acc_gate, out_gate, g_all, 0)
-    rows1.when_owner(rows1.ring.s01)
-    rows1.when_owner(rows1.ring.tm10)
-    weight_tile(1, acc_gate, out_gate, g_all, 1)
-    store(out_gate, grad_gate)
-    weight_tile(1, acc_up, out_up, u_all, 0)
-    weight_tile(1, acc_up, out_up, u_all, 1)
-    store(out_up, grad_up)
-    finish(rows1)
+    R0, R1 = ColReduce(0), ColReduce(1)
+    Q0, Q1 = RowReduce(0), RowReduce(1)
+
+    W.start()
+    count_send(0)
+    loads["gs"].wait()
+    loads["us"].wait()
+    hidden(0, H0)
+    hidden(1, H1)
+    loads["inputs"].wait()
+    in_all[row] = jnp.transpose(in_own[...].astype(F32)).astype(BF)
+    W.z1()
+    count_recv(0)
+    count_send(1)
+    W.f1()
+    H0.f1()
+    W.g1()
+    H0.z1()
+    H1.f1()
+    W.rest()
+    H0.g1()
+    H1.z1()
+    W.last()
+    count_recv(1)
+    count_send(2)
+    H0.rest()
+    H0.last()
+    W.sib()
+    H1.g1()
+    loads["dw"].wait()
+    R0.c(0)
+    R0.c(1)
+    count_recv(2)
+    count_send(3)
+    R0.c(2)
+    R0.c(3)
+    R1.c(0)
+    H1.rest()
+    I.start()
+    R1.c(1)
+    R1.c(2)
+    H1.last()
+    R1.c(3)
+    count_recv(3)
+    down(0)
+    down(1)
+    R0.s01()
+    down(2)
+    R0.t20()
+    I.f1()
+    down(3)
+    R1.t20()
+    R1.s01()
+    I.z1()
+    R0.tm10()
+    R1.tm10()
+    I.g1()
+    hidden_grads(0, R0, G0)
+    U0.start()
+    I.rest()
+    hidden_grads(1, R1, G1)
+    U1.start()
+    I.last()
+    G0.f1()
+    I.sib()
+    G0.z1()
+    U0.f1()
+    U0.z1()
+    G1.f1()
+    G1.z1()
+    U1.f1()
+    U1.z1()
+    G0.g1()
+    G0.rest()
+    G0.last()
+    weight(0, 0, g_all, acc_gate, out_gate, grad_gate)
+    U0.g1()
+    weight(0, 1, g_all, acc_gate, out_gate, grad_gate)
+    loads["gw"].wait()
+    loads["uw"].wait()
+    Q0.a(0)
+    Q0.a(1)
+    Q0.a(2)
+    Q0.a(3)
+    U0.rest()
+    U0.last()
+    Q0.c(0)
+    G1.g1()
+    Q0.c(1)
+    Q0.c(2)
+    Q0.c(3)
+    weight(0, 0, u_all, acc_up, out_up, grad_up)
+    Q0.k(0)
+    Q0.k(1)
+    weight(0, 1, u_all, acc_up, out_up, grad_up)
+    Q0.k(2)
+    Q0.k(3)
+    G1.rest()
+    G1.last()
+    Q1.a(0)
+    U1.g1()
+    Q1.a(1)
+    Q1.a(2)
+    Q0.s01()
+    Q1.a(3)
+    Q0.t20()
+    weight(1, 0, g_all, acc_gate, out_gate, grad_gate)
+    weight(1, 1, g_all, acc_gate, out_gate, grad_gate)
+    U1.rest()
+    U1.last()
+    Q1.c(0)
+    Q0.tm10()
+    Q1.c(1)
+    Q1.c(2)
+    Q1.c(3)
+    Q1.k(0)
+    weight(1, 0, u_all, acc_up, out_up, grad_up)
+    Q1.k(1)
+    Q0.fin()
+    Q1.k(2)
+    weight(1, 1, u_all, acc_up, out_up, grad_up)
+    Q1.k(3)
+    Q1.t20()
+    Q1.s01()
+    Q1.tm10()
+    Q1.fin()
     last = pltpu.make_async_copy(out_in, grad_input, local_sems.at[3])
     last.start()
     wire.drain()
-    rows0.drain()
-    rows1.drain()
+    Q0.drain()
+    Q1.drain()
     for copy in stores:
         copy.wait()
     last.wait()
     assert wire.count == N_MESSAGES, wire.count
 
 
+def move(*refs):
+    sources, results, held, sems = refs[:4], refs[4:8], refs[8:12], refs[12]
+    pieces = []
+    for array in range(4):
+        rows = sources[array].shape[0] // 2
+        for part in range(2):
+            at = pl.ds(part * rows, rows)
+            number = 2 * (2 * array + part)
+            load = pltpu.make_async_copy(
+                sources[array].at[at], held[array].at[at], sems.at[number]
+            )
+            save = pltpu.make_async_copy(
+                held[array].at[at], results[array].at[at], sems.at[number + 1]
+            )
+            pieces.append((load, save))
+    for load, _ in pieces:
+        load.start()
+    for load, save in pieces:
+        load.wait()
+        save.start()
+    for _, save in pieces:
+        save.wait()
+
+
 def shards(
     inputs, upstream, mask_flags, levels, gate_saved, up_saved, gate_weight, up_weight, down_weight
 ):
     anywhere = pl.BlockSpec(memory_space=pl.ANY)
-    return pl.pallas_call(
+    results = (
+        jax.ShapeDtypeStruct((128, 1024), BF),
+        jax.ShapeDtypeStruct((1024, 896), BF),
+        jax.ShapeDtypeStruct((1024, 896), BF),
+        jax.ShapeDtypeStruct((896, 1024), BF),
+    )
+    grads = pl.pallas_call(
         kernel,
-        out_shape=(
-            jax.ShapeDtypeStruct((128, 1024), BF),
-            jax.ShapeDtypeStruct((1024, 896), BF),
-            jax.ShapeDtypeStruct((1024, 896), BF),
-            jax.ShapeDtypeStruct((896, 1024), BF),
-        ),
+        out_shape=results,
         in_specs=[
             pl.BlockSpec(memory_space=pltpu.SMEM),
             pl.BlockSpec(memory_space=pltpu.VMEM),
@@ -585,6 +646,7 @@
             pltpu.VMEM((2, 8, 128, 1024), BF),
             pltpu.VMEM((8, 128, 1024), BF),
             pltpu.VMEM((7, 128, 1024), BF),
+            pltpu.VMEM((4, 256, 1024), F32),
             pltpu.VMEM((1024, 896), F32),
             pltpu.VMEM((1024, 896), F32),
             pltpu.VMEM((1024, 896), BF),
@@ -614,6 +676,16 @@
         up_weight,
         down_weight,
     )
+    return pl.pallas_call(
+        move,
+        out_shape=results,
+        in_specs=[anywhere] * 4,
+        out_specs=(anywhere,) * 4,
+        scratch_shapes=[pltpu.VMEM(result.shape, BF) for result in results]
+        + [pltpu.SemaphoreType.DMA((16,))],
+        compiler_params=pltpu.CompilerParams(vmem_limit_bytes=62 * 2**20),
+        name="move_results",
+    )(*grads)
 
 
 def solution(mesh):

time: 180 us -> 147 us (0.82)
  Pallas kernels: 171 us -> 147 us
  local copies, waits for them, and re-layouts: 8.07 us -> 0 us
    pallas_call x1 -> x2, Pallas kernels: 171 us -> 147 us  [the longest x1 141 us: shards(): pl.pallas_call(kernel, out_shape=results, in_specs=[pl.BlockSpec(memory_s...]
    unnamed x8 -> x0, local copies, waits for them, and re-layouts: 8.07 us -> none
where the time goes in v2:
time: 147 us
  Pallas kernels  147 us (100%)
    pallas_call x1, Pallas kernels, shards(): pl.pallas_call(kernel, out_shape=results, in_specs=[pl.BlockSpec(memory_s...  141 us
    pallas_call x1, Pallas kernels, shards(): pl.pallas_call(move, out_shape=results, in_specs=[anywhere] * 4, out_spec...  5.19 us

profile of v2, /device:TPU:1, one launch (start us, length us, event | category | flops | bytes accessed | tf_op | source)
XLA Modules:
  0.0 147.4 jit_solution(12174771298201877960)
XLA Ops:
  0.6 141.4 %swiglu_backward.1 = (bf16[128,1024]{1,0:T(8,128)(2,1)}, bf16[1024,896]{1,0:T(8,128)(2,1)}, bf16[1024,896]{1,0:T(8,128)(2,1)}, bf16[896,1024]{1,0:T(8,128)(2,1)}) custom-call(s32[4]{0:T(128)} %levels.1, s32[1,128]{1,0:T(1,128)} %bitcast.1, bf16[128,1024]{1,0:T(8,128)(2,1)} %inputs.1, bf16[128,1024]{1,0:T(8,128)(2,1)} %upstream.1, ...), custom_call_target="tpu_custom_call" | custom-call | flops 22548578304 | bytes 16777216 | tf_op jit(solution)/shard_map/swiglu_backward/pallas_call | solution.py:622
  142.0 5.2 %move_results.1 = (bf16[128,1024]{1,0:T(8,128)(2,1)}, bf16[1024,896]{1,0:T(8,128)(2,1)}, bf16[1024,896]{1,0:T(8,128)(2,1)}, bf16[896,1024]{1,0:T(8,128)(2,1)}) custom-call(bf16[128,1024]{1,0:T(8,128)(2,1)} %get-tuple-element.8.refs_0_, bf16[1024,896]{1,0:T(8,128)(2,1)} %get-tuple-element.9.refs_1_, bf16[1024,896]{1,0:T(8,128)(2,1)} %get-tuple-element.10.refs_2_, ...), custom_call_target="tpu_custom_call" | custom-call | tf_op jit(solution)/shard_map/move_results/pallas_call | solution.py:679

commit v3 on v2

--- a/solution.py
+++ b/solution.py
@@ -10,6 +10,7 @@
 F32 = jnp.float32
 MESH = pl.DeviceIdType.MESH
 NT = (((1,), (1,)), ((), ()))
+MIRROR = (0, 1, 3, 2, 5, 4, 6, 7)
 ORDER = ((2, 1), (2, 0), (1, 1), (-1, 1), (1, 0), (-1, 0), (0, 1), (0, 0))
 
 
@@ -33,27 +34,28 @@
             device_id_type=MESH,
         )
 
-    def send(self, number, src, dst, device, keep=True):
+    def send(self, number, src, dst, device):
         self.copy(number, src, dst, device).start()
-        if keep:
-            self.sent.append((number, src, dst, device))
+        self.sent.append((number, src, dst, device))
 
     def recv(self, number, dst):
         self.copy(number, dst, dst, self.anyone).wait_recv()
 
-    def drain(self):
-        for message in self.sent:
+    def drain(self, numbers=None):
+        chosen = [m for m in self.sent if numbers is None or m[0] in numbers]
+        self.sent = [m for m in self.sent if m not in chosen]
+        for message in chosen:
             self.copy(*message).wait_send()
 
 
 class Gather:
     def __init__(
-        self, wire, buf, slot, minus, plus, across, sibling=None, other_slot=None, far_z=True
+        self, wire, at, minus, plus, across, sibling=None, other_at=None, far_z=True
     ):
         self.far_z = far_z
-        self.wire, self.buf, self.slot = wire, buf, slot
+        self.wire, self.at = wire, at
         self.minus, self.plus, self.across = minus, plus, across
-        self.sibling, self.other_slot = sibling, other_slot
+        self.sibling, self.other_at = sibling, other_at
         self.ids = {
             name: wire.new()
             for name in ("own_m", "own_p", "own_z", "z_m", "z_p", "fwd_p", "far")
@@ -61,16 +63,16 @@
         self.sib_ids = {d: wire.new() for d in ORDER} if sibling is not None else {}
 
     def push(self, name, d, device):
-        ref = self.buf.at[self.slot(d)]
+        ref = self.at(d)
         self.wire.send(self.ids[name], ref, ref, device)
 
     def share(self, d):
         if self.sibling is not None:
-            ref = self.buf.at[self.slot(d)]
+            ref = self.at(d)
             self.wire.send(self.sib_ids[d], ref, ref, self.sibling)
 
     def take(self, name, d):
-        self.wire.recv(self.ids[name], self.buf.at[self.slot(d)])
+        self.wire.recv(self.ids[name], self.at(d))
 
     def start(self):
         self.push("own_z", (0, 0), self.across)
@@ -117,36 +119,27 @@
 
     def sib(self):
         for d in ORDER:
-            self.wire.recv(self.sib_ids[d], self.buf.at[self.other_slot(d)])
+            self.wire.recv(self.sib_ids[d], self.other_at(d))
 
 
 class Reduce:
-    def __init__(self, wire, part, got, minus, plus, across, keep=True):
+    def __init__(self, wire, part, got, minus, plus, across):
         self.wire, self.part, self.got = wire, part, got
-        self.minus, self.plus, self.across, self.keep = minus, plus, across, keep
+        self.minus, self.plus, self.across = minus, plus, across
         self.ids = [wire.new() for _ in range(7)]
-        self.log = []
 
     def push(self, index, d, device):
-        src = self.part.at[ORDER.index(d)]
-        message = (self.ids[index], src, self.got.at[index], device)
-        self.wire.send(*message, keep=self.keep)
-        self.log.append((index, d, device))
-
-    def drain(self):
-        for index, d, device in self.log:
-            src = self.part.at[ORDER.index(d)]
-            self.wire.copy(self.ids[index], src, self.got.at[index], device).wait_send()
+        self.wire.send(self.ids[index], self.part(ORDER.index(d)), self.got.at[index], device)
 
     def add(self, d, *indices):
-        term = self.part[ORDER.index(d)].astype(F32)
+        term = self.part(ORDER.index(d))[...].astype(F32)
         for index in indices:
             self.wire.recv(self.ids[index], self.got.at[index])
             term = term + self.got[index].astype(F32)
         return term
 
     def store(self, d, term):
-        self.part[ORDER.index(d)] = term.astype(BF)
+        self.part(ORDER.index(d))[...] = term.astype(BF)
 
     def p0(self):
         self.push(0, (2, 1), self.across)
@@ -174,7 +167,7 @@
         return self.add((0, 0), 4, 6, 5)
 
 
-N_MESSAGES = 2 * 15 + 3 * 2 * 7 + 2 * 7 + 2 * (8 + 7) + 4
+N_MESSAGES = 3 * 15 + 3 * 2 * 7 + 2 * 7 + 2 * (8 + 7) + 4
 N_LOCAL = 10
 
 
@@ -210,6 +203,7 @@
     q_sib,
     q_got,
     q_acc,
+    acc_down,
     acc_gate,
     acc_up,
     out_gate,
@@ -241,11 +235,14 @@
     def flip(bit, d):
         return 1 - bit if d else bit
 
+    def chip_at(d):
+        return flip(z_lo, d[1]) * 4 + lax.rem(x + sign * d[0] + 8, 4)
+
     def row_slot(d, k=core):
-        return row_of(flip(z_lo, d[1]), x + sign * d[0], k)
-
-    def col_slot(d, half):
-        return 2 * col_of(y + sign * d[0], flip(z_hi, d[1])) + half
+        return 2 * chip_at(d) + k
+
+    def col_at(d):
+        return col_of(y + sign * d[0], flip(z_hi, d[1]))
 
     loads = {}
     for number, (name, src, dst) in enumerate(
@@ -277,16 +274,28 @@
     pl.semaphore_wait(barrier, len(neighbours))
 
     wire = Wire(send_sems, recv_sems, sibling)
-    def row_gather(buf, far_z):
+    def row_gather(view, far_z):
         return Gather(
-            wire, buf, row_slot, row_m, row_p, row_z, sibling, lambda d: row_slot(d, 1 - core), far_z
+            wire,
+            lambda d: view(row_slot(d)),
+            row_m,
+            row_p,
+            row_z,
+            sibling,
+            lambda d: view(row_slot(d, 1 - core)),
+            far_z,
         )
 
-    def col_gather(buf, half):
-        return Gather(wire, buf, lambda d: col_slot(d, half), col_m, col_p, col_z)
-
-    W, I = row_gather(w_all, False), row_gather(in_all, False)
-    H0, H1 = (col_gather(h_all, half) for half in range(2))
+    def col_gather(buf, half, far_z=True):
+        def at(d):
+            return buf.at[2 * col_at(d) + half]
+
+        return Gather(wire, at, col_m, col_p, col_z, far_z=far_z)
+
+    W0 = row_gather(lambda slot: w_all.at[slot, pl.ds(0, 64)], False)
+    W1 = row_gather(lambda slot: w_all.at[slot, pl.ds(64, 64)], False)
+    I = row_gather(lambda slot: in_all.at[slot], False)
+    H0, H1 = col_gather(h_all, 0), col_gather(h_all, 1, False)
     G0, G1 = (col_gather(g_all, half) for half in range(2))
     U0, U1 = (col_gather(u_all, half) for half in range(2))
 
@@ -306,26 +315,30 @@
         wire.recv(count_ids[stage], count.at[2 * stage + 1])
         count[2 * stage + 2] = count[2 * stage] + count[2 * stage + 1]
 
-    def saved(half):
-        gate_f = gs[pl.ds(half * 128, 128), :].astype(F32)
-        up_f = us[pl.ds(half * 128, 128), :].astype(F32)
+    def saved(parts):
+        gate_f = jnp.concatenate([gs[at, :] for at in parts], axis=0).astype(F32)
+        up_f = jnp.concatenate([us[at, :] for at in parts], axis=0).astype(F32)
         sigmoid_gate = jax.nn.sigmoid(gate_f)
         return gate_f, up_f, sigmoid_gate, sigmoid_gate * gate_f
 
-    def hidden(half, gather):
-        _, up_f, _, silu_gate = saved(half)
+    def hidden(half):
+        _, up_f, _, silu_gate = saved([pl.ds(half * 128, 128)])
         values = (silu_gate * up_f).astype(BF).astype(F32)
         h_all[2 * col + half] = jnp.transpose(values).astype(BF)
-        gather.start()
 
     class ColReduce(Reduce):
         def __init__(self, half):
             self.half = half
-            super().__init__(wire, h_part.at[half], h_got.at[half], col_m, col_p, col_z)
+            super().__init__(
+                wire, lambda index: h_part.at[half, index], h_got.at[half], col_m, col_p, col_z
+            )
 
         def c(self, pair):
             ds = ORDER[2 * pair : 2 * pair + 2]
-            rows = jnp.concatenate([w_all[col_slot(d, self.half)] for d in ds], axis=0)
+            at = pl.ds(64 * self.half, 64)
+            rows = jnp.concatenate(
+                [w_all[2 * col_at(d) + k, at, :] for d in ds for k in range(2)], axis=0
+            )
             term = lax.dot_general(rows, dw[...], NT, preferred_element_type=F32).astype(BF)
             h_part[self.half, 2 * pair] = term[:128]
             h_part[self.half, 2 * pair + 1] = term[128:]
@@ -335,7 +348,9 @@
     def hidden_grads(half, reduce, gather):
         scale = 2048.0 / count[8][0:1, 0:1]
         hidden_grad = scale * reduce.final()
-        gate_f, up_f, sigmoid_gate, silu_gate = saved(half)
+        gate_f, up_f, sigmoid_gate, silu_gate = saved(
+            [pl.ds(128 * k + 64 * half, 64) for k in range(2)]
+        )
         g_all[2 * col + half] = (
             hidden_grad * up_f * sigmoid_gate * (1.0 + gate_f * (1.0 - sigmoid_gate))
         ).astype(BF)
@@ -348,17 +363,28 @@
         stores.append(pltpu.make_async_copy(src, dst, local_sems.at[7 + len(stores)]))
         stores[-1].start()
 
-    def down(tile):
-        scale = 2048.0 / count[8][0:1, 0:1]
+    def down(half, tile):
         at = pl.ds(tile * 224, 224)
-        lhs = jnp.concatenate([h_all[slot, at, :] for slot in range(16)], axis=1)
-        rhs = jnp.concatenate([w_all[slot] for slot in range(16)], axis=0)
-        out_down[at, :] = (scale * jnp.dot(lhs, rhs, preferred_element_type=F32)).astype(BF)
-        if tile == 3:
-            store(out_down, grad_down)
+        lhs = jnp.concatenate([h_all[2 * c + half, at, :] for c in range(8)], axis=1)
+        rhs = jnp.concatenate([w_all[2 * c + half] for c in range(8)], axis=0)
+        term = jnp.dot(lhs, rhs, preferred_element_type=F32)
+        if half == 0:
+            acc_down[at, :] = term
+        else:
+            scale = 2048.0 / count[8][0:1, 0:1]
+            out_down[at, :] = (scale * (acc_down[at, :] + term)).astype(BF)
+            if tile == 3:
+                store(out_down, grad_down)
+
+    def regroup():
+        wire.drain(list(I.ids.values()) + list(I.sib_ids.values()))
+        for c in range(8):
+            first, second = in_all[2 * c], in_all[2 * c + 1]
+            in_all[2 * c] = jnp.concatenate([first[:, :64], second[:, :64]], axis=1)
+            in_all[2 * c + 1] = jnp.concatenate([first[:, 64:], second[:, 64:]], axis=1)
 
     def weight(half, tile, grads, acc, out, result):
-        at = pl.ds(tile * 512, 512)
+        at = pl.ds(tile * 256, 256)
         lhs = jnp.concatenate([in_all[2 * c + half, at, :] for c in range(8)], axis=1)
         rhs = jnp.concatenate([grads[2 * c + half] for c in range(8)], axis=0)
         term = jnp.dot(lhs, rhs, preferred_element_type=F32)
@@ -366,23 +392,24 @@
             acc[at, :] = term
         else:
             out[at, :] = (acc[at, :] + term).astype(BF)
-            if tile == 1:
+            if tile == 3:
                 store(out, result)
 
-    class RowReduce:
+    class RowReduce(Reduce):
         def __init__(self, half):
             self.half = half
-            self.ids = [wire.new() for _ in ORDER]
-            self.ring = Reduce(wire, q_part.at[half], q_got, row_m, row_p, row_z, keep=False)
-
-        def when_owner(self, do):
-            pl.when(core == self.half)(do)
+            self.sib_ids = [wire.new() for _ in ORDER]
+            super().__init__(
+                wire,
+                lambda index: q_part.at[half, index, core],
+                q_got.at[half],
+                row_m,
+                row_p,
+                row_z,
+            )
 
         def rows(self, grads, pair):
-            slots = [
-                row_of(flip(z_lo, d[1]), x + (1 - 2 * self.half) * d[0], self.half)
-                for d in ORDER[2 * pair : 2 * pair + 2]
-            ]
+            slots = [2 * chip_at(d) + self.half for d in ORDER[2 * pair : 2 * pair + 2]]
             return jnp.concatenate([grads[slot] for slot in slots], axis=0)
 
         def a(self, pair):
@@ -394,191 +421,183 @@
             term = q_acc[pair] + lax.dot_general(
                 self.rows(u_all, pair), uw[...], NT, preferred_element_type=F32
             )
-            q_part[self.half, 2 * pair] = term[:128].astype(BF)
-            q_part[self.half, 2 * pair + 1] = term[128:].astype(BF)
-
-            @pl.when(core != self.half)
-            def _():
-                for index in (2 * pair, 2 * pair + 1):
-                    wire.send(
-                        self.ids[index],
-                        q_part.at[self.half, index],
-                        q_sib.at[index],
-                        sibling,
-                        keep=False,
-                    )
+            for part in range(4):
+                q_part[self.half, 2 * pair + part // 2, part % 2] = term[
+                    64 * part : 64 * part + 64
+                ].astype(BF)
+            for index in (2 * pair, 2 * pair + 1):
+                there = MIRROR[index]
+                wire.send(
+                    self.sib_ids[there],
+                    q_part.at[self.half, index, 1 - core],
+                    q_sib.at[self.half, there],
+                    sibling,
+                )
 
         def k(self, pair):
-            def do():
-                for index in (2 * pair, 2 * pair + 1):
-                    wire.recv(self.ids[index], q_sib.at[index])
-                    q_part[self.half, index] = (
-                        q_part[self.half, index].astype(F32) + q_sib[index].astype(F32)
-                    ).astype(BF)
-                if pair < 3:
-                    (self.ring.p0, self.ring.p1, self.ring.p2)[pair]()
-
-            self.when_owner(do)
-
-        def t20(self):
-            self.when_owner(self.ring.t20)
-
-        def tm10(self):
-            self.when_owner(self.ring.tm10)
-
-        def s01(self):
-            self.when_owner(self.ring.s01)
+            for index in (2 * pair, 2 * pair + 1):
+                wire.recv(self.sib_ids[index], q_sib.at[self.half, index])
+                own = self.part(index)
+                own[...] = (
+                    own[...].astype(F32) + q_sib[self.half, index].astype(F32)
+                ).astype(BF)
+            if pair < 3:
+                (self.p0, self.p1, self.p2)[pair]()
 
         def fin(self):
-            def do():
-                out_in[...] = self.ring.final().astype(BF)
-
-            self.when_owner(do)
-
-        def drain(self):
-            @pl.when(core != self.half)
-            def _():
-                for index in range(8):
-                    wire.copy(
-                        self.ids[index],
-                        q_part.at[self.half, index],
-                        q_sib.at[index],
-                        sibling,
-                    ).wait_send()
-
-            self.when_owner(self.ring.drain)
+            out_in[pl.ds(64 * self.half, 64), :] = self.final().astype(BF)
 
     R0, R1 = ColReduce(0), ColReduce(1)
     Q0, Q1 = RowReduce(0), RowReduce(1)
 
-    W.start()
+    W0.start()
     count_send(0)
+    loads["inputs"].wait()
+    in_all[row] = jnp.transpose(in_own[...].astype(F32)).astype(BF)
     loads["gs"].wait()
     loads["us"].wait()
-    hidden(0, H0)
-    hidden(1, H1)
-    loads["inputs"].wait()
-    in_all[row] = jnp.transpose(in_own[...].astype(F32)).astype(BF)
-    W.z1()
+    hidden(1)
+    hidden(0)
+    H0.start()
+    W0.z1()
     count_recv(0)
     count_send(1)
-    W.f1()
+    W0.f1()
+    W0.g1()
+    W1.start()
+    W0.rest()
+    H0.z1()
     H0.f1()
-    W.g1()
-    H0.z1()
-    H1.f1()
-    W.rest()
-    H0.g1()
-    H1.z1()
-    W.last()
+    W0.last()
     count_recv(1)
     count_send(2)
-    H0.rest()
-    H0.last()
-    W.sib()
-    H1.g1()
+    W1.z1()
+    W0.sib()
+    W1.f1()
     loads["dw"].wait()
     R0.c(0)
     R0.c(1)
     count_recv(2)
     count_send(3)
+    W1.g1()
     R0.c(2)
+    W1.rest()
+    H0.rest()
     R0.c(3)
+    H0.g1()
+    W1.last()
+    R0.t20()
+    W1.sib()
     R1.c(0)
-    H1.rest()
-    I.start()
     R1.c(1)
     R1.c(2)
-    H1.last()
     R1.c(3)
-    count_recv(3)
-    down(0)
-    down(1)
     R0.s01()
-    down(2)
-    R0.t20()
-    I.f1()
-    down(3)
+    H0.last()
+    down(0, 0)
+    down(0, 1)
+    R0.tm10()
+    I.start()
+    down(0, 2)
+    down(0, 3)
     R1.t20()
     R1.s01()
+    I.f1()
+    count_recv(3)
+    hidden_grads(0, R0, G0)
+    R1.tm10()
     I.z1()
-    R0.tm10()
-    R1.tm10()
+    G0.f1()
+    U0.start()
     I.g1()
-    hidden_grads(0, R0, G0)
-    U0.start()
-    I.rest()
     hidden_grads(1, R1, G1)
     U1.start()
+    I.rest()
+    G0.g1()
+    G0.z1()
     I.last()
-    G0.f1()
     I.sib()
-    G0.z1()
+    regroup()
     U0.f1()
     U0.z1()
     G1.f1()
     G1.z1()
     U1.f1()
     U1.z1()
-    G0.g1()
+    H1.start()
     G0.rest()
     G0.last()
-    weight(0, 0, g_all, acc_gate, out_gate, grad_gate)
-    U0.g1()
-    weight(0, 1, g_all, acc_gate, out_gate, grad_gate)
     loads["gw"].wait()
     loads["uw"].wait()
     Q0.a(0)
     Q0.a(1)
     Q0.a(2)
+    U0.g1()
     Q0.a(3)
+    weight(0, 0, g_all, acc_gate, out_gate, grad_gate)
+    weight(0, 1, g_all, acc_gate, out_gate, grad_gate)
+    weight(0, 2, g_all, acc_gate, out_gate, grad_gate)
+    H1.z1()
+    weight(0, 3, g_all, acc_gate, out_gate, grad_gate)
     U0.rest()
+    G1.g1()
     U0.last()
     Q0.c(0)
-    G1.g1()
     Q0.c(1)
     Q0.c(2)
     Q0.c(3)
+    Q0.k(0)
     weight(0, 0, u_all, acc_up, out_up, grad_up)
-    Q0.k(0)
     Q0.k(1)
+    Q0.k(2)
+    G1.rest()
     weight(0, 1, u_all, acc_up, out_up, grad_up)
-    Q0.k(2)
     Q0.k(3)
-    G1.rest()
+    weight(0, 2, u_all, acc_up, out_up, grad_up)
     G1.last()
+    weight(1, 0, g_all, acc_gate, out_gate, grad_gate)
+    U1.g1()
+    weight(1, 1, g_all, acc_gate, out_gate, grad_gate)
+    weight(1, 2, g_all, acc_gate, out_gate, grad_gate)
+    Q0.t20()
+    weight(1, 3, g_all, acc_gate, out_gate, grad_gate)
     Q1.a(0)
-    U1.g1()
+    weight(0, 3, u_all, acc_up, out_up, grad_up)
     Q1.a(1)
+    U1.rest()
+    Q0.tm10()
     Q1.a(2)
-    Q0.s01()
     Q1.a(3)
-    Q0.t20()
-    weight(1, 0, g_all, acc_gate, out_gate, grad_gate)
-    weight(1, 1, g_all, acc_gate, out_gate, grad_gate)
-    U1.rest()
     U1.last()
     Q1.c(0)
-    Q0.tm10()
     Q1.c(1)
     Q1.c(2)
     Q1.c(3)
     Q1.k(0)
+    H1.f1()
+    Q0.s01()
+    Q1.k(1)
     weight(1, 0, u_all, acc_up, out_up, grad_up)
-    Q1.k(1)
+    Q1.k(2)
+    Q1.k(3)
+    H1.g1()
+    weight(1, 1, u_all, acc_up, out_up, grad_up)
+    weight(1, 2, u_all, acc_up, out_up, grad_up)
+    weight(1, 3, u_all, acc_up, out_up, grad_up)
+    Q1.t20()
+    H1.rest()
+    Q1.s01()
     Q0.fin()
-    Q1.k(2)
-    weight(1, 1, u_all, acc_up, out_up, grad_up)
-    Q1.k(3)
-    Q1.t20()
-    Q1.s01()
     Q1.tm10()
+    H1.last()
+    down(1, 0)
+    down(1, 1)
+    down(1, 2)
     Q1.fin()
+    down(1, 3)
     last = pltpu.make_async_copy(out_in, grad_input, local_sems.at[3])
     last.start()
     wire.drain()
-    Q0.drain()
-    Q1.drain()
     for copy in stores:
         copy.wait()
     last.wait()
@@ -643,10 +662,11 @@
             pltpu.VMEM((256, 896), BF),
             pltpu.VMEM((2, 8, 128, 896), BF),
             pltpu.VMEM((2, 7, 128, 896), BF),
-            pltpu.VMEM((2, 8, 128, 1024), BF),
-            pltpu.VMEM((8, 128, 1024), BF),
-            pltpu.VMEM((7, 128, 1024), BF),
+            pltpu.VMEM((2, 8, 2, 64, 1024), BF),
+            pltpu.VMEM((2, 8, 64, 1024), BF),
+            pltpu.VMEM((2, 7, 64, 1024), BF),
             pltpu.VMEM((4, 256, 1024), F32),
+            pltpu.VMEM((896, 1024), F32),
             pltpu.VMEM((1024, 896), F32),
             pltpu.VMEM((1024, 896), F32),
             pltpu.VMEM((1024, 896), BF),

time: 147 us -> 139 us (0.946); the launches traced: 147 us -> 137 us
  Pallas kernels: 147 us -> 136 us
    pallas_call x1, Pallas kernels: 141 us -> 131 us  [shards(): pl.pallas_call(kernel, out_shape=results, in_specs=[pl.BlockSpec(memory_s...]
where the time goes in v3:
time: 139 us; the launch traced here: 137 us
  Pallas kernels  136 us (98%)
    pallas_call x1, Pallas kernels, shards(): pl.pallas_call(kernel, out_shape=results, in_specs=[pl.BlockSpec(memory_s...  131 us
    pallas_call x1, Pallas kernels, shards(): pl.pallas_call(move, out_shape=results, in_specs=[anywhere] * 4, out_spec...  5.19 us

profile of v3, /device:TPU:1, one launch (start us, length us, event | category | flops | bytes accessed | tf_op | source)
XLA Modules:
  0.0 137.2 jit_solution(14568185534355768362)
XLA Ops:
  0.6 131.2 %swiglu_backward.1 = (bf16[128,1024]{1,0:T(8,128)(2,1)}, bf16[1024,896]{1,0:T(8,128)(2,1)}, bf16[1024,896]{1,0:T(8,128)(2,1)}, bf16[896,1024]{1,0:T(8,128)(2,1)}) custom-call(s32[4]{0:T(128)} %levels.1, s32[1,128]{1,0:T(1,128)} %bitcast.1, bf16[128,1024]{1,0:T(8,128)(2,1)} %inputs.1, bf16[128,1024]{1,0:T(8,128)(2,1)} %upstream.1, ...), custom_call_target="tpu_custom_call" | custom-call | flops 22548578304 | bytes 16777216 | tf_op jit(solution)/shard_map/swiglu_backward/pallas_call | solution.py:641
  131.8 5.2 %move_results.1 = (bf16[128,1024]{1,0:T(8,128)(2,1)}, bf16[1024,896]{1,0:T(8,128)(2,1)}, bf16[1024,896]{1,0:T(8,128)(2,1)}, bf16[896,1024]{1,0:T(8,128)(2,1)}) custom-call(bf16[128,1024]{1,0:T(8,128)(2,1)} %get-tuple-element.8.refs_0_, bf16[1024,896]{1,0:T(8,128)(2,1)} %get-tuple-element.9.refs_1_, bf16[1024,896]{1,0:T(8,128)(2,1)} %get-tuple-element.10.refs_2_, ...), custom_call_target="tpu_custom_call" | custom-call | tf_op jit(solution)/shard_map/move_results/pallas_call | solution.py:699

commit v4 on v3

--- a/solution.py
+++ b/solution.py
@@ -168,7 +168,7 @@
 
 
 N_MESSAGES = 3 * 15 + 3 * 2 * 7 + 2 * 7 + 2 * (8 + 7) + 4
-N_LOCAL = 10
+N_LOCAL = 7
 
 
 def kernel(
@@ -181,10 +181,10 @@
     gate_weight,
     up_weight,
     down_weight,
-    grad_input,
-    grad_gate,
-    grad_up,
-    grad_down,
+    out_in,
+    out_gate,
+    out_up,
+    out_down,
     w_all,
     in_all,
     h_all,
@@ -206,10 +206,6 @@
     acc_down,
     acc_gate,
     acc_up,
-    out_gate,
-    out_up,
-    out_down,
-    out_in,
     count,
     send_sems,
     recv_sems,
@@ -235,14 +231,19 @@
     def flip(bit, d):
         return 1 - bit if d else bit
 
-    def chip_at(d):
-        return flip(z_lo, d[1]) * 4 + lax.rem(x + sign * d[0] + 8, 4)
+    def chip_at(d, turned=False):
+        step = -d[0] if turned else d[0]
+        return flip(z_lo, d[1]) * 4 + lax.rem(x + sign * step + 8, 4)
 
     def row_slot(d, k=core):
         return 2 * chip_at(d) + k
 
-    def col_at(d):
-        return col_of(y + sign * d[0], flip(z_hi, d[1]))
+    def col_at(d, turned=False):
+        step = -d[0] if turned else d[0]
+        return col_of(y + sign * step, flip(z_hi, d[1]))
+
+    def ring(minus, plus, turned):
+        return (plus, minus) if turned else (minus, plus)
 
     loads = {}
     for number, (name, src, dst) in enumerate(
@@ -286,18 +287,21 @@
             far_z,
         )
 
-    def col_gather(buf, half, far_z=True):
+    def col_gather(buf, half, far_z, turned):
         def at(d):
-            return buf.at[2 * col_at(d) + half]
-
-        return Gather(wire, at, col_m, col_p, col_z, far_z=far_z)
+            return buf.at[2 * col_at(d, turned) + half]
+
+        return Gather(wire, at, *ring(col_m, col_p, turned), col_z, far_z=far_z)
 
     W0 = row_gather(lambda slot: w_all.at[slot, pl.ds(0, 64)], False)
     W1 = row_gather(lambda slot: w_all.at[slot, pl.ds(64, 64)], False)
     I = row_gather(lambda slot: in_all.at[slot], False)
-    H0, H1 = col_gather(h_all, 0), col_gather(h_all, 1, False)
-    G0, G1 = (col_gather(g_all, half) for half in range(2))
-    U0, U1 = (col_gather(u_all, half) for half in range(2))
+    H0 = col_gather(h_all, 0, False, True)
+    H1 = col_gather(h_all, 1, False, True)
+    G0 = col_gather(g_all, 0, True, False)
+    G1 = col_gather(g_all, 1, True, False)
+    U0 = col_gather(u_all, 0, True, True)
+    U1 = col_gather(u_all, 1, True, False)
 
     step = 1 - 2 * lax.rem(x, 2)
     partners = (
@@ -327,17 +331,21 @@
         h_all[2 * col + half] = jnp.transpose(values).astype(BF)
 
     class ColReduce(Reduce):
-        def __init__(self, half):
-            self.half = half
+        def __init__(self, half, turned):
+            self.half, self.turned = half, turned
             super().__init__(
-                wire, lambda index: h_part.at[half, index], h_got.at[half], col_m, col_p, col_z
+                wire,
+                lambda index: h_part.at[half, index],
+                h_got.at[half],
+                *ring(col_m, col_p, turned),
+                col_z,
             )
 
         def c(self, pair):
             ds = ORDER[2 * pair : 2 * pair + 2]
             at = pl.ds(64 * self.half, 64)
             rows = jnp.concatenate(
-                [w_all[2 * col_at(d) + k, at, :] for d in ds for k in range(2)], axis=0
+                [w_all[2 * col_at(d, self.turned) + k, at, :] for d in ds for k in range(2)], axis=0
             )
             term = lax.dot_general(rows, dw[...], NT, preferred_element_type=F32).astype(BF)
             h_part[self.half, 2 * pair] = term[:128]
@@ -357,12 +365,6 @@
         gather.start()
         u_all[2 * col + half] = (hidden_grad * silu_gate).astype(BF)
 
-    stores = []
-
-    def store(src, dst):
-        stores.append(pltpu.make_async_copy(src, dst, local_sems.at[7 + len(stores)]))
-        stores[-1].start()
-
     def down(half, tile):
         at = pl.ds(tile * 224, 224)
         lhs = jnp.concatenate([h_all[2 * c + half, at, :] for c in range(8)], axis=1)
@@ -373,8 +375,6 @@
         else:
             scale = 2048.0 / count[8][0:1, 0:1]
             out_down[at, :] = (scale * (acc_down[at, :] + term)).astype(BF)
-            if tile == 3:
-                store(out_down, grad_down)
 
     def regroup():
         wire.drain(list(I.ids.values()) + list(I.sib_ids.values()))
@@ -383,7 +383,7 @@
             in_all[2 * c] = jnp.concatenate([first[:, :64], second[:, :64]], axis=1)
             in_all[2 * c + 1] = jnp.concatenate([first[:, 64:], second[:, 64:]], axis=1)
 
-    def weight(half, tile, grads, acc, out, result):
+    def weight(half, tile, grads, acc, out):
         at = pl.ds(tile * 256, 256)
         lhs = jnp.concatenate([in_all[2 * c + half, at, :] for c in range(8)], axis=1)
         rhs = jnp.concatenate([grads[2 * c + half] for c in range(8)], axis=0)
@@ -392,24 +392,22 @@
             acc[at, :] = term
         else:
             out[at, :] = (acc[at, :] + term).astype(BF)
-            if tile == 3:
-                store(out, result)
 
     class RowReduce(Reduce):
-        def __init__(self, half):
-            self.half = half
+        def __init__(self, half, turned):
+            self.half, self.turned = half, turned
             self.sib_ids = [wire.new() for _ in ORDER]
             super().__init__(
                 wire,
                 lambda index: q_part.at[half, index, core],
                 q_got.at[half],
-                row_m,
-                row_p,
+                *ring(row_m, row_p, turned),
                 row_z,
             )
 
         def rows(self, grads, pair):
-            slots = [2 * chip_at(d) + self.half for d in ORDER[2 * pair : 2 * pair + 2]]
+            ds = ORDER[2 * pair : 2 * pair + 2]
+            slots = [2 * chip_at(d, self.turned) + self.half for d in ds]
             return jnp.concatenate([grads[slot] for slot in slots], axis=0)
 
         def a(self, pair):
@@ -447,8 +445,8 @@
         def fin(self):
             out_in[pl.ds(64 * self.half, 64), :] = self.final().astype(BF)
 
-    R0, R1 = ColReduce(0), ColReduce(1)
-    Q0, Q1 = RowReduce(0), RowReduce(1)
+    R0, R1 = ColReduce(0, False), ColReduce(1, False)
+    Q0, Q1 = RowReduce(0, True), RowReduce(1, False)
 
     W0.start()
     count_send(0)
@@ -456,176 +454,147 @@
     in_all[row] = jnp.transpose(in_own[...].astype(F32)).astype(BF)
     loads["gs"].wait()
     loads["us"].wait()
-    hidden(1)
     hidden(0)
     H0.start()
+    W1.start()
+    hidden(1)
     W0.z1()
     count_recv(0)
     count_send(1)
+    H1.start()
     W0.f1()
+    H0.f1()
     W0.g1()
-    W1.start()
+    W1.f1()
+    H0.z1()
     W0.rest()
-    H0.z1()
-    H0.f1()
+    W1.z1()
     W0.last()
     count_recv(1)
     count_send(2)
-    W1.z1()
     W0.sib()
-    W1.f1()
     loads["dw"].wait()
     R0.c(0)
+    H0.g1()
+    W1.rest()
+    W1.g1()
+    I.start()
     R0.c(1)
     count_recv(2)
     count_send(3)
-    W1.g1()
+    W1.last()
+    H0.rest()
+    R0.t20()
     R0.c(2)
-    W1.rest()
-    H0.rest()
+    W1.sib()
     R0.c(3)
-    H0.g1()
-    W1.last()
-    R0.t20()
-    W1.sib()
+    H0.last()
     R1.c(0)
     R1.c(1)
+    I.z1()
     R1.c(2)
-    R1.c(3)
     R0.s01()
-    H0.last()
-    down(0, 0)
     down(0, 1)
     R0.tm10()
-    I.start()
+    R1.c(3)
+    down(0, 3)
+    I.f1()
+    I.g1()
+    R1.t20()
     down(0, 2)
-    down(0, 3)
-    R1.t20()
-    R1.s01()
-    I.f1()
     count_recv(3)
     hidden_grads(0, R0, G0)
+    U0.start()
+    R1.s01()
+    down(0, 0)
     R1.tm10()
-    I.z1()
     G0.f1()
-    U0.start()
-    I.g1()
-    hidden_grads(1, R1, G1)
-    U1.start()
     I.rest()
-    G0.g1()
     G0.z1()
     I.last()
     I.sib()
+    U0.f1()
     regroup()
-    U0.f1()
+    G0.g1()
     U0.z1()
-    G1.f1()
-    G1.z1()
-    U1.f1()
-    U1.z1()
-    H1.start()
+    hidden_grads(1, R1, G1)
     G0.rest()
     G0.last()
+    weight(0, 3, g_all, acc_gate, out_gate)
+    weight(0, 1, g_all, acc_gate, out_gate)
     loads["gw"].wait()
     loads["uw"].wait()
     Q0.a(0)
+    U0.g1()
+    U1.start()
     Q0.a(1)
     Q0.a(2)
-    U0.g1()
-    Q0.a(3)
-    weight(0, 0, g_all, acc_gate, out_gate, grad_gate)
-    weight(0, 1, g_all, acc_gate, out_gate, grad_gate)
-    weight(0, 2, g_all, acc_gate, out_gate, grad_gate)
-    H1.z1()
-    weight(0, 3, g_all, acc_gate, out_gate, grad_gate)
+    G1.f1()
     U0.rest()
-    G1.g1()
+    weight(0, 2, g_all, acc_gate, out_gate)
     U0.last()
     Q0.c(0)
+    U1.f1()
     Q0.c(1)
+    Q0.k(0)
+    Q0.a(3)
+    G1.z1()
     Q0.c(2)
+    U1.z1()
+    weight(0, 1, u_all, acc_up, out_up)
+    G1.g1()
     Q0.c(3)
-    Q0.k(0)
-    weight(0, 0, u_all, acc_up, out_up, grad_up)
+    H1.z1()
+    Q0.k(2)
+    H1.f1()
+    weight(0, 0, u_all, acc_up, out_up)
     Q0.k(1)
-    Q0.k(2)
+    weight(0, 3, u_all, acc_up, out_up)
+    Q0.k(3)
+    weight(0, 2, u_all, acc_up, out_up)
+    weight(0, 0, g_all, acc_gate, out_gate)
+    U1.g1()
+    Q0.t20()
     G1.rest()
-    weight(0, 1, u_all, acc_up, out_up, grad_up)
-    Q0.k(3)
-    weight(0, 2, u_all, acc_up, out_up, grad_up)
     G1.last()
-    weight(1, 0, g_all, acc_gate, out_gate, grad_gate)
-    U1.g1()
-    weight(1, 1, g_all, acc_gate, out_gate, grad_gate)
-    weight(1, 2, g_all, acc_gate, out_gate, grad_gate)
-    Q0.t20()
-    weight(1, 3, g_all, acc_gate, out_gate, grad_gate)
     Q1.a(0)
-    weight(0, 3, u_all, acc_up, out_up, grad_up)
     Q1.a(1)
-    U1.rest()
-    Q0.tm10()
+    Q0.s01()
     Q1.a(2)
     Q1.a(3)
+    weight(1, 0, g_all, acc_gate, out_gate)
+    U1.rest()
     U1.last()
     Q1.c(0)
     Q1.c(1)
     Q1.c(2)
+    Q0.tm10()
+    Q1.k(0)
+    weight(1, 0, u_all, acc_up, out_up)
+    Q1.k(1)
+    H1.g1()
+    weight(1, 1, g_all, acc_gate, out_gate)
     Q1.c(3)
-    Q1.k(0)
-    H1.f1()
-    Q0.s01()
-    Q1.k(1)
-    weight(1, 0, u_all, acc_up, out_up, grad_up)
+    weight(1, 1, u_all, acc_up, out_up)
+    H1.rest()
+    Q1.t20()
     Q1.k(2)
+    Q0.fin()
+    weight(1, 2, u_all, acc_up, out_up)
+    weight(1, 3, u_all, acc_up, out_up)
     Q1.k(3)
-    H1.g1()
-    weight(1, 1, u_all, acc_up, out_up, grad_up)
-    weight(1, 2, u_all, acc_up, out_up, grad_up)
-    weight(1, 3, u_all, acc_up, out_up, grad_up)
-    Q1.t20()
-    H1.rest()
     Q1.s01()
-    Q0.fin()
-    Q1.tm10()
     H1.last()
     down(1, 0)
+    Q1.tm10()
+    weight(1, 2, g_all, acc_gate, out_gate)
+    weight(1, 3, g_all, acc_gate, out_gate)
     down(1, 1)
     down(1, 2)
+    down(1, 3)
     Q1.fin()
-    down(1, 3)
-    last = pltpu.make_async_copy(out_in, grad_input, local_sems.at[3])
-    last.start()
     wire.drain()
-    for copy in stores:
-        copy.wait()
-    last.wait()
     assert wire.count == N_MESSAGES, wire.count
-
-
-def move(*refs):
-    sources, results, held, sems = refs[:4], refs[4:8], refs[8:12], refs[12]
-    pieces = []
-    for array in range(4):
-        rows = sources[array].shape[0] // 2
-        for part in range(2):
-            at = pl.ds(part * rows, rows)
-            number = 2 * (2 * array + part)
-            load = pltpu.make_async_copy(
-                sources[array].at[at], held[array].at[at], sems.at[number]
-            )
-            save = pltpu.make_async_copy(
-                held[array].at[at], results[array].at[at], sems.at[number + 1]
-            )
-            pieces.append((load, save))
-    for load, _ in pieces:
-        load.start()
-    for load, save in pieces:
-        load.wait()
-        save.start()
-    for _, save in pieces:
-        save.wait()
 
 
 def shards(
@@ -638,15 +607,16 @@
         jax.ShapeDtypeStruct((1024, 896), BF),
         jax.ShapeDtypeStruct((896, 1024), BF),
     )
-    grads = pl.pallas_call(
+    inside = pl.BlockSpec(memory_space=pltpu.VMEM)
+    return pl.pallas_call(
         kernel,
-        out_shape=results,
+        out_shape=tuple(pltpu.VMEM(result.shape, BF) for result in results),
         in_specs=[
             pl.BlockSpec(memory_space=pltpu.SMEM),
             pl.BlockSpec(memory_space=pltpu.VMEM),
         ]
         + [anywhere] * 7,
-        out_specs=(anywhere,) * 4,
+        out_specs=(inside,) * 4,
         scratch_shapes=[
             pltpu.VMEM((16, 128, 1024), BF),
             pltpu.VMEM((16, 1024, 128), BF),
@@ -669,17 +639,13 @@
             pltpu.VMEM((896, 1024), F32),
             pltpu.VMEM((1024, 896), F32),
             pltpu.VMEM((1024, 896), F32),
-            pltpu.VMEM((1024, 896), BF),
-            pltpu.VMEM((1024, 896), BF),
-            pltpu.VMEM((896, 1024), BF),
-            pltpu.VMEM((128, 1024), BF),
             pltpu.VMEM((9, 8, 128), F32),
             pltpu.SemaphoreType.DMA((N_MESSAGES,)),
             pltpu.SemaphoreType.DMA((N_MESSAGES,)),
             pltpu.SemaphoreType.DMA((N_LOCAL,)),
         ],
         compiler_params=pltpu.CompilerParams(
-            collective_id=0, has_side_effects=True, vmem_limit_bytes=62 * 2**20
+            collective_id=0, has_side_effects=True, vmem_limit_bytes=56 * 2**20
         ),
         cost_estimate=pl.CostEstimate(
             flops=12 * 2048 * 1024 * 896, bytes_accessed=16 * 2**20, transcendentals=2 * 256 * 896
@@ -696,16 +662,6 @@
         up_weight,
         down_weight,
     )
-    return pl.pallas_call(
-        move,
-        out_shape=results,
-        in_specs=[anywhere] * 4,
-        out_specs=(anywhere,) * 4,
-        scratch_shapes=[pltpu.VMEM(result.shape, BF) for result in results]
-        + [pltpu.SemaphoreType.DMA((16,))],
-        compiler_params=pltpu.CompilerParams(vmem_limit_bytes=62 * 2**20),
-        name="move_results",
-    )(*grads)
 
 
 def solution(mesh):

time: 139 us -> 129 us (0.928); the launches traced: 137 us -> 129 us
  Pallas kernels: 136 us -> 124 us
  local copies, waits for them, and re-layouts: 0 us -> 4.39 us
    pallas_call x2 -> x1, Pallas kernels: 136 us -> 124 us  [shards(): pl.pallas_call(kernel, out_shape=tuple((pltpu.VMEM(result.shape, BF) for...]
    unnamed x0 -> x4, local copies, waits for them, and re-layouts: none -> 4.39 us
where the time goes in v4:
time: 129 us
  Pallas kernels  124 us (96%)
  local copies, waits for them, and re-layouts  4.39 us (3%)
    pallas_call x1, Pallas kernels, shards(): pl.pallas_call(kernel, out_shape=tuple((pltpu.VMEM(result.shape, BF) for...  124 us
    unnamed x4, local copies, waits for them, and re-layouts  4.39 us

profile of v4, /device:TPU:1, one launch (start us, length us, event | category | flops | bytes accessed | tf_op | source)
XLA Modules:
  0.0 129.3 jit_solution(13669591938057489732)
XLA Ops:
  0.6 124.3 %swiglu_backward.1 = (bf16[128,1024]{1,0:T(8,128)(2,1)S(1)}, bf16[1024,896]{1,0:T(8,128)(2,1)S(1)}, bf16[1024,896]{1,0:T(8,128)(2,1)S(1)}, bf16[896,1024]{1,0:T(8,128)(2,1)S(1)}) custom-call(s32[4]{0:T(128)} %levels.1, s32[1,128]{1,0:T(1,128)} %bitcast.1, bf16[128,1024]{1,0:T(8,128)(2,1)} %inputs.1, bf16[128,1024]{1,0:T(8,128)(2,1)} %upstream.1, ...), custom_call_target="tpu_custom_call" | custom-call | flops 22548578304 | bytes 16777216 | tf_op jit(solution)/shard_map/swiglu_backward/pallas_call | solution.py:611
  124.9 0.7 copy.17
  125.6 1.2 copy.18
  126.9 1.2 copy.19
  128.1 1.2 copy.20

commit v5 on v4

--- a/solution.py
+++ b/solution.py
@@ -597,6 +597,24 @@
     assert wire.count == N_MESSAGES, wire.count
 
 
+def move(*refs):
+    sources, results, sems = refs[:4], refs[4:8], refs[8]
+    saves = []
+    for array in range(4):
+        rows = sources[array].shape[0] // 2
+        for part in range(2):
+            at = pl.ds(part * rows, rows)
+            saves.append(
+                pltpu.make_async_copy(
+                    sources[array].at[at], results[array].at[at], sems.at[2 * array + part]
+                )
+            )
+    for save in saves:
+        save.start()
+    for save in saves:
+        save.wait()
+
+
 def shards(
     inputs, upstream, mask_flags, levels, gate_saved, up_saved, gate_weight, up_weight, down_weight
 ):
@@ -608,7 +626,7 @@
         jax.ShapeDtypeStruct((896, 1024), BF),
     )
     inside = pl.BlockSpec(memory_space=pltpu.VMEM)
-    return pl.pallas_call(
+    grads = pl.pallas_call(
         kernel,
         out_shape=tuple(pltpu.VMEM(result.shape, BF) for result in results),
         in_specs=[
@@ -662,6 +680,15 @@
         up_weight,
         down_weight,
     )
+    return pl.pallas_call(
+        move,
+        out_shape=results,
+        in_specs=[inside] * 4,
+        out_specs=(anywhere,) * 4,
+        scratch_shapes=[pltpu.SemaphoreType.DMA((8,))],
+        compiler_params=pltpu.CompilerParams(vmem_limit_bytes=56 * 2**20),
+        name="move_results",
+    )(*[pltpu.with_memory_space_constraint(grad, pltpu.VMEM) for grad in grads])
 
 
 def solution(mesh):

time: 129 us -> 128 us (level)
  local copies, waits for them, and re-layouts: 4.39 us -> 0 us
  Pallas kernels: 124 us -> 127 us
    unnamed x4 -> x0, local copies, waits for them, and re-layouts: 4.39 us -> none
    pallas_call x0 -> x1, Pallas kernels: none -> 2.59 us  [shards(): pl.pallas_call(move, out_shape=results, in_specs=[inside] * 4, out_specs=...]
where the time goes in v5:
time: 128 us
  Pallas kernels  127 us (99%)
    pallas_call x1, Pallas kernels, shards(): pl.pallas_call(kernel, out_shape=tuple((pltpu.VMEM(result.shape, BF) for...  124 us
    pallas_call x1, Pallas kernels, shards(): pl.pallas_call(move, out_shape=results, in_specs=[inside] * 4, out_specs=...  2.59 us

profile of v5, /device:TPU:1, one launch (start us, length us, event | category | flops | bytes accessed | tf_op | source)
XLA Modules:
  0.0 127.7 jit_solution(6340346785075369686)
XLA Ops:
  0.6 124.3 %swiglu_backward.1 = (bf16[128,1024]{1,0:T(8,128)(2,1)S(1)}, bf16[1024,896]{1,0:T(8,128)(2,1)S(1)}, bf16[1024,896]{1,0:T(8,128)(2,1)S(1)}, bf16[896,1024]{1,0:T(8,128)(2,1)S(1)}) custom-call(s32[4]{0:T(128)} %levels.1, s32[1,128]{1,0:T(1,128)} %bitcast.1, bf16[128,1024]{1,0:T(8,128)(2,1)} %inputs.1, bf16[128,1024]{1,0:T(8,128)(2,1)} %upstream.1, ...), custom_call_target="tpu_custom_call" | custom-call | flops 22548578304 | bytes 16777216 | tf_op jit(solution)/shard_map/swiglu_backward/pallas_call | solution.py:629
  124.9 2.6 %move_results.1 = (bf16[128,1024]{1,0:T(8,128)(2,1)}, bf16[1024,896]{1,0:T(8,128)(2,1)}, bf16[1024,896]{1,0:T(8,128)(2,1)}, bf16[896,1024]{1,0:T(8,128)(2,1)}) custom-call(bf16[128,1024]{1,0:T(8,128)(2,1)S(1)} %get-tuple-element.8.refs_0_, bf16[1024,896]{1,0:T(8,128)(2,1)S(1)} %get-tuple-element.9.refs_1_, bf16[1024,896]{1,0:T(8,128)(2,1)S(1)} %get-tuple-element.10.refs_2_, ...), custom_call_target="tpu_custom_call" | custom-call | tf_op jit(solution)/shard_map/move_results/pallas_call | solution.py:683

commit v6 on v5

--- a/solution.py
+++ b/solution.py
@@ -269,7 +269,14 @@
     noise = jnp.full((1, 128), levels[row * 128 // SEQ], jnp.int32).astype(F32) / 1000.0
     factor = flags / noise
     loads["upstream"].wait()
-    w_all[row] = (up_own[...].astype(F32) * jnp.concatenate([factor] * 8, axis=1)).astype(BF)
+
+    def weigh(at):
+        spread = jnp.concatenate([factor[at : at + 64]] * 8, axis=1)
+        w_all[row, pl.ds(at, 64), :] = (
+            up_own[pl.ds(at, 64), :].astype(F32) * spread
+        ).astype(BF)
+
+    weigh(0)
     count[0] = jnp.broadcast_to(jnp.sum(flags, axis=0, keepdims=True), (8, 128))
 
     pl.semaphore_wait(barrier, len(neighbours))
@@ -449,6 +456,7 @@
     Q0, Q1 = RowReduce(0, True), RowReduce(1, False)
 
     W0.start()
+    weigh(64)
     count_send(0)
     loads["inputs"].wait()
     in_all[row] = jnp.transpose(in_own[...].astype(F32)).astype(BF)

time: 128 us -> 128 us (level)
  no operation moved by 1% of the time
where the time goes in v6:
time: 128 us
  Pallas kernels  127 us (99%)
    pallas_call x1, Pallas kernels, shards(): pl.pallas_call(kernel, out_shape=tuple((pltpu.VMEM(result.shape, BF) for...  124 us
    pallas_call x1, Pallas kernels, shards(): pl.pallas_call(move, out_shape=results, in_specs=[inside] * 4, out_specs=...  2.59 us

profile of v6, /device:TPU:1, one launch (start us, length us, event | category | flops | bytes accessed | tf_op | source)
XLA Modules:
  0.0 127.7 jit_solution(5270436917319217795)
XLA Ops:
  0.6 124.3 %swiglu_backward.1 = (bf16[128,1024]{1,0:T(8,128)(2,1)S(1)}, bf16[1024,896]{1,0:T(8,128)(2,1)S(1)}, bf16[1024,896]{1,0:T(8,128)(2,1)S(1)}, bf16[896,1024]{1,0:T(8,128)(2,1)S(1)}) custom-call(s32[4]{0:T(128)} %levels.1, s32[1,128]{1,0:T(1,128)} %bitcast.1, bf16[128,1024]{1,0:T(8,128)(2,1)} %inputs.1, bf16[128,1024]{1,0:T(8,128)(2,1)} %upstream.1, ...), custom_call_target="tpu_custom_call" | custom-call | flops 22548578304 | bytes 16777216 | tf_op jit(solution)/shard_map/swiglu_backward/pallas_call | solution.py:637
  124.9 2.6 %move_results.1 = (bf16[128,1024]{1,0:T(8,128)(2,1)}, bf16[1024,896]{1,0:T(8,128)(2,1)}, bf16[1024,896]{1,0:T(8,128)(2,1)}, bf16[896,1024]{1,0:T(8,128)(2,1)}) custom-call(bf16[128,1024]{1,0:T(8,128)(2,1)S(1)} %get-tuple-element.8.refs_0_, bf16[1024,896]{1,0:T(8,128)(2,1)S(1)} %get-tuple-element.9.refs_1_, bf16[1024,896]{1,0:T(8,128)(2,1)S(1)} %get-tuple-element.10.refs_2_, ...), custom_call_target="tpu_custom_call" | custom-call | tf_op jit(solution)/shard_map/move_results/pallas_call | solution.py:691
